TPU v7x, 512 devices: a whole 4x4x16 slice. The times are simulated.
512 devices in a mesh: dp: 32 (over x, z_hi, y), expert: 16 (over z_lo, core).
Axes of the slice: x: 4, y: 4, z: 16 (z_hi: 2, z_lo: 8; z = z_hi * 8 + z_lo), core: 2. Of those that a mesh axis runs over, the one named last changes fastest.
Arguments:
- tokens: bfloat16 [65536, 1280], P(('dp', 'expert')), may hold values from -12 to 12
- out_grad: bfloat16 [65536, 1280], P(('dp', 'expert')), may hold values from -6 to 6
- slot_param: bfloat16 [1280, 128], replicated, may hold values from -1 to 1
- w_in: bfloat16 [512, 640, 1280], P(('dp', 'expert')), may hold values from -0.15625 to 0.15625
- w_out: bfloat16 [512, 640, 1280], P(('dp', 'expert')), may hold values from -0.125 to 0.125
Outputs:
- token_grad: bfloat16 [65536, 1280], P(('dp', 'expert'))
- param_grad: bfloat16 [1280, 128], P('dp', 'expert')
All inputs are finite; a program needn't handle non-finite values.
Results may differ from a plain program's by a relative error of at most 0.018.
Values may be sent and summed in bfloat16 or wider, within the bound.
A program may use at most 64 MiB of HBM per device.

v0:
```python
import jax
import jax.numpy as jnp
from jax import lax
from jax.sharding import PartitionSpec as P

gelu_scale = 0.7978845608
gelu_cubic = 0.044715


def from_partner(block, axis, stride):
    count = lax.axis_size(axis)
    route = []
    for low in range(count):
        high = low | 1 << stride
        if high != low and high < count:
            route += [(low, high), (high, low)]
    return lax.ppermute(block, axis, route)


def gelu_parts(pre_act):
    inner_arg = gelu_scale * (pre_act + gelu_cubic * pre_act * pre_act * pre_act)
    tangent = jnp.tanh(inner_arg)
    gelu_value = 0.5 * pre_act * (1.0 + tangent)
    gelu_slope = 0.5 * (1.0 + tangent) + 0.5 * pre_act * (1.0 - tangent * tangent) * gelu_scale * (
        1.0 + 3.0 * gelu_cubic * pre_act * pre_act
    )
    return (gelu_value, gelu_slope)


def shards(tokens, out_grad, slot_param, w_in, w_out):
    ranks = lax.axis_size("dp")
    ranks_ex = lax.axis_size("expert")
    experts = slot_param.shape[1]
    width = tokens.shape[1]
    quarter = width // 4
    images = ranks * ranks_ex // 2
    position = lax.axis_index("expert")
    logits = jnp.dot(tokens, slot_param, preferred_element_type=jnp.float32)
    local_max = jnp.max(logits, axis=0)
    col_max = jnp.maximum(local_max, from_partner(local_max, "expert", 0))
    half_sum = jnp.sum(jnp.exp(logits - col_max), axis=0)
    col_sum = half_sum + from_partner(half_sum, "expert", 0)
    dispatch = jnp.exp(logits - col_max) / col_sum
    row_exp = jnp.exp(logits - jnp.max(logits, axis=1, keepdims=True))
    combine = row_exp / jnp.sum(row_exp, axis=1, keepdims=True)
    dispatch_b = dispatch.astype(jnp.bfloat16)
    combine_b = combine.astype(jnp.bfloat16)
    slot_in_part = jnp.einsum("te,td->ed", dispatch_b, tokens, preferred_element_type=jnp.float32)
    slot_grad_part = jnp.einsum(
        "te,td->ed", combine_b, out_grad, preferred_element_type=jnp.float32
    )
    in_blocks = slot_in_part.reshape(ranks, ranks_ex, quarter)
    grad_blocks = slot_grad_part.reshape(ranks, ranks_ex, quarter)
    recv_in, recv_grad = (
        lax.all_to_all(
            lax.all_to_all(in_blocks, "dp", split_axis=0, concat_axis=0, tiled=True),
            "expert",
            split_axis=1,
            concat_axis=1,
            tiled=True,
        ),
        lax.all_to_all(
            lax.all_to_all(grad_blocks, "dp", split_axis=0, concat_axis=0, tiled=True),
            "expert",
            split_axis=1,
            concat_axis=1,
            tiled=True,
        ),
    )
    slot_in_cols = (
        jnp.sum(recv_in.reshape(ranks, ranks_ex // 2, 2, quarter), axis=2)
        .reshape(images, quarter)
        .astype(jnp.bfloat16)
    )
    slot_grad_cols = (
        jnp.sum(recv_grad.reshape(ranks, ranks_ex // 2, 2, quarter), axis=2)
        .reshape(images, quarter)
        .astype(jnp.bfloat16)
    )
    whole_in = slot_in_cols
    whole_grad = slot_grad_cols
    for bit in range(2):
        other_in, other_grad = from_partner((whole_in, whole_grad), "expert", bit)
        upper = position // (1 << bit) % 2 == 1
        whole_in = jnp.where(
            upper,
            jnp.concatenate([other_in, whole_in], 1),
            jnp.concatenate([whole_in, other_in], 1),
        )
        whole_grad = jnp.where(
            upper,
            jnp.concatenate([other_grad, whole_grad], 1),
            jnp.concatenate([whole_grad, other_grad], 1),
        )
    first = w_in[0]
    second = w_out[0]
    pre_act = jnp.einsum("nd,fd->nf", whole_in, first, preferred_element_type=jnp.float32)
    gelu_value, gelu_slope = gelu_parts(pre_act)
    out_part = jnp.dot(gelu_value.astype(jnp.bfloat16), second, preferred_element_type=jnp.float32)
    hidden_grad = jnp.einsum("nd,fd->nf", whole_grad, second, preferred_element_type=jnp.float32)
    pre_grad = (hidden_grad * gelu_slope).astype(jnp.bfloat16)
    back_part = jnp.dot(pre_grad, first, preferred_element_type=jnp.float32)
    for bit in (1, 0):
        span = out_part.shape[1] // 2
        upper = position // (1 << bit) % 2 == 1
        keep_out = jnp.where(upper, out_part[:, span:], out_part[:, :span])
        give_out = jnp.where(upper, out_part[:, :span], out_part[:, span:])
        keep_back = jnp.where(upper, back_part[:, span:], back_part[:, :span])
        give_back = jnp.where(upper, back_part[:, :span], back_part[:, span:])
        got_out, got_back = from_partner((give_out, give_back), "expert", bit)
        out_part = keep_out + got_out
        back_part = keep_back + got_back

    def spread(rows):
        blocks = rows.astype(jnp.bfloat16).reshape(ranks, ranks_ex // 2, 1, quarter)
        return jnp.broadcast_to(blocks, (ranks, ranks_ex // 2, 2, quarter)).reshape(
            ranks, ranks_ex, quarter
        )

    back_out, back_in = (
        lax.all_to_all(
            lax.all_to_all(spread(out_part), "dp", split_axis=0, concat_axis=0, tiled=True),
            "expert",
            split_axis=1,
            concat_axis=1,
            tiled=True,
        ),
        lax.all_to_all(
            lax.all_to_all(spread(back_part), "dp", split_axis=0, concat_axis=0, tiled=True),
            "expert",
            split_axis=1,
            concat_axis=1,
            tiled=True,
        ),
    )
    slot_out = back_out.reshape(experts, width)
    slot_in_grad = back_in.reshape(experts, width)
    comb_grad = jnp.einsum("td,ed->te", out_grad, slot_out, preferred_element_type=jnp.float32)
    disp_grad = jnp.einsum("td,ed->te", tokens, slot_in_grad, preferred_element_type=jnp.float32)
    disp_local = jnp.sum(dispatch * disp_grad, axis=0)
    disp_inner = disp_local + from_partner(disp_local, "expert", 0)
    comb_inner = jnp.sum(combine * comb_grad, axis=1, keepdims=True)
    logit_grad = (combine * (comb_grad - comb_inner) + dispatch * (disp_grad - disp_inner)).astype(
        jnp.bfloat16
    )
    token_grad = (
        jnp.dot(dispatch_b, slot_in_grad, preferred_element_type=jnp.float32)
        + jnp.einsum("te,de->td", logit_grad, slot_param, preferred_element_type=jnp.float32)
    ).astype(jnp.bfloat16)
    param_rows = lax.psum_scatter(
        jnp.einsum("td,te->de", tokens, logit_grad, preferred_element_type=jnp.float32),
        "dp",
        scatter_dimension=0,
        tiled=True,
    )
    param_grad = lax.psum_scatter(param_rows, "expert", scatter_dimension=1, tiled=True).astype(
        jnp.bfloat16
    )
    return (token_grad, param_grad)


def solution(mesh):
    placed = (
        P(("dp", "expert"), None),
        P(("dp", "expert"), None),
        P(),
        P(("dp", "expert"), None, None),
        P(("dp", "expert"), None, None),
    )
    return jax.shard_map(
        shards,
        mesh=mesh,
        in_specs=placed,
        out_specs=(P(("dp", "expert"), None), P("dp", "expert")),
        check_vma=False,
    )
```

profile of v0, /device:TPU:1, one launch (start us, length us, event | category | flops | bytes accessed | tf_op | source)
XLA Modules:
  0.0 1044.8 jit_solution(5311123342899938047)
XLA Ops:
  7.2 1.5 fusion.84
  8.7 8.8 collective-permute-start
  18.5 2.2 collective-permute-start.1
  21.5 1.3 fusion.67
  22.8 1.2 reshape.44
  24.0 14.9 %all-to-all-start.2 = ((f32[32,16,320]{2,1,0:T(8,128)}), f32[32,16,320]{2,1,0:T(8,128)S(1)}, u32[]{:S(2)}, u32[]{:S(2)}) async-start(f32[32,16,320]{2,1,0:T(8,128)} %reshape.44), calls=%async_computation.2 | async-start | bytes 1572864 | tf_op jit(solution)/shard_map/all_to_all | solution.py:56
  39.3 1.2 reshape.42
  40.6 25.4 %all-to-all-done.2 = f32[32,16,320]{2,1,0:T(8,128)S(1)} async-done(((f32[32,16,320]{2,1,0:T(8,128)}), f32[32,16,320]{2,1,0:T(8,128)S(1)}, u32[]{:S(2)}, u32[]{:S(2)}) %all-to-all-start.2) | async-done | bytes 655392 | tf_op jit(solution)/shard_map/all_to_all | solution.py:56
  65.9 4.6 all-to-all-start
  70.6 1.2 copy.29
  71.7 19.4 %all-to-all-done = f32[32,16,320]{2,1,0:T(8,128)} async-done(((f32[32,16,320]{2,1,0:T(8,128)}), f32[32,16,320]{2,1,0:T(8,128)}, u32[]{:S(2)}, u32[]{:S(2)}) %all-to-all-start) | async-done | bytes 655392 | tf_op jit(solution)/shard_map/all_to_all | solution.py:63
  91.2 37.6 %all-to-all-start.3 = ((f32[32,16,320]{2,0,1:T(8,128)}), f32[32,16,320]{2,0,1:T(8,128)S(1)}, u32[]{:S(2)}, u32[]{:S(2)}) async-start(f32[32,16,320]{2,0,1:T(8,128)} %copy.29), calls=%async_computation.3 | async-start | bytes 1572864 | tf_op jit(solution)/shard_map/all_to_all | solution.py:55
  128.8 2.3 copy.27
  131.0 33.0 %all-to-all-done.3 = f32[32,16,320]{2,0,1:T(8,128)S(1)} async-done(((f32[32,16,320]{2,0,1:T(8,128)}), f32[32,16,320]{2,0,1:T(8,128)S(1)}, u32[]{:S(2)}, u32[]{:S(2)}) %all-to-all-start.3) | async-done | bytes 655392 | tf_op jit(solution)/shard_map/all_to_all | solution.py:55
  164.0 9.1 all-to-all-start.1
  173.3 2.0 collective-permute-start.4
  175.3 33.1 %all-to-all-done.1 = f32[32,16,320]{2,0,1:T(8,128)S(1)} async-done(((f32[32,16,320]{2,0,1:T(8,128)}), f32[32,16,320]{2,0,1:T(8,128)S(1)}, u32[]{:S(2)}, u32[]{:S(2)}) %all-to-all-start.1) | async-done | bytes 655392 | tf_op jit(solution)/shard_map/all_to_all | solution.py:62
  208.6 1.9 collective-permute-start.2
  210.8 5.5 collective-permute-start.5
  216.5 1.9 collective-permute-start.3
  218.4 5.4 collective-permute-done.5
  223.9 3.0 fusion.3
  226.9 4.1 collective-permute-done.3
  231.0 3.2 fusion.1
  235.3 3.0 collective-permute-start.6
  239.1 13.2 %collective-permute-done.6 = f32[256,640]{1,0:T(8,128)S(1)} collective-permute-done((f32[256,640]{1,0:T(8,128)S(1)}, f32[256,640]{1,0:T(8,128)S(1)}, u32[]{:S(2)}, u32[]{:S(2)}) %collective-permute-start.6) | collective-permute-done | bytes 655392 | tf_op jit(solution)/shard_map/ppermute | solution.py:17
  252.6 3.9 collective-permute-start.7
  257.4 3.0 collective-permute-start.8
  261.9 11.4 %all-to-all-start.4 = ((bf16[32,16,320]{2,1,0:T(8,128)(2,1)}), bf16[32,16,320]{2,1,0:T(8,128)(2,1)S(1)}, u32[]{:S(2)}, u32[]{:S(2)}) async-start(bf16[32,16,320]{2,1,0:T(8,128)(2,1)} %reshape.46), calls=%async_computation.4 | async-start | bytes 786432 | tf_op jit(solution)/shard_map/all_to_all | solution.py:129
  273.3 2.7 collective-permute-done.8
  276.0 1.2 select_add_fusion
  277.3 3.1 collective-permute-start.9
  280.4 1.3 collective-permute-done.9
  283.2 8.4 all-to-all-done.4
  291.6 5.0 all-to-all-start.6
  297.5 16.3 %all-to-all-done.6 = bf16[32,16,320]{2,1,0:T(8,128)(2,1)S(1)} async-done(((bf16[32,16,320]{2,1,0:T(8,128)(2,1)}), bf16[32,16,320]{2,1,0:T(8,128)(2,1)S(1)}, u32[]{:S(2)}, u32[]{:S(2)}) %all-to-all-start.6) | async-done | bytes 327712 | tf_op jit(solution)/shard_map/all_to_all | solution.py:122
  313.8 26.8 %all-to-all-start.5 = ((bf16[32,16,320]{2,0,1:T(8,128)(2,1)}), bf16[32,16,320]{2,0,1:T(8,128)(2,1)S(1)}, u32[]{:S(2)}, u32[]{:S(2)}) async-start(bf16[32,16,320]{2,0,1:T(8,128)(2,1)} %copy.31), calls=%async_computation.5 | async-start | bytes 786432 | tf_op jit(solution)/shard_map/all_to_all | solution.py:128
  341.4 20.8 %all-to-all-done.5 = bf16[32,16,320]{2,0,1:T(8,128)(2,1)S(1)} async-done(((bf16[32,16,320]{2,0,1:T(8,128)(2,1)}), bf16[32,16,320]{2,0,1:T(8,128)(2,1)S(1)}, u32[]{:S(2)}, u32[]{:S(2)}) %all-to-all-start.5) | async-done | bytes 327712 | tf_op jit(solution)/shard_map/all_to_all | solution.py:128
  362.2 6.2 all-to-all-start.7
  369.2 20.8 %all-to-all-done.7 = bf16[32,16,320]{2,0,1:T(8,128)(2,1)S(1)} async-done(((bf16[32,16,320]{2,0,1:T(8,128)(2,1)}), bf16[32,16,320]{2,0,1:T(8,128)(2,1)S(1)}, u32[]{:S(2)}, u32[]{:S(2)}) %all-to-all-start.7) | async-done | bytes 327712 | tf_op jit(solution)/shard_map/all_to_all | solution.py:121
  390.5 1.4 multiply_reduce_fusion.1
  391.9 1.9 collective-permute-start.10
  393.8 1.1 collective-permute-done.10
  394.9 1.2 convolution_bitcast_fusion
  396.2 1.3 dynamic-slice
  397.4 1.3 dynamic-slice.2
  401.3 533.4 %all-reduce.4.cloned.1.call-done = f32[1280,128]{0,1:T(8,128)} async-done(((f32[1280,128]{0,1:T(8,128)}), f32[1280,128]{0,1:T(8,128)}) %all-reduce.4.cloned.1.call-update) | async-done | bytes 655376
  935.7 101.7 %all-reduce.1 = bf16[40,128]{0,1:T(8,128)(2,1)S(1)} all-reduce(f32[40,128]{0,1:T(8,128)S(1)} %constant_dynamic-slice_fusion), channel_id=3, replica_groups=mesh['dp'=32,'expert'=16] {'expert'}, use_global_device_ids=true, to_apply=%region_9.10.clone | all-reduce | flops 5120 | bytes 30720
  (55 shorter events, 14.7 us)
Async XLA Ops:
  7.2 223.8 %copy-start = (bf16[1,640,1280]{2,1,0:T(8,128)(2,1)S(1)}, bf16[1,640,1280]{2,1,0:T(8,128)(2,1)}, u32[]{:S(2)}) copy-start(bf16[1,640,1280]{2,1,0:T(8,128)(2,1)} %param.9) | copy-start | bytes 4915204
  8.7 9.6 collective-permute-start
  18.5 3.0 collective-permute-start.1
  22.7 16.2 %copy-start.6 = (bf16[128,1280]{1,0:T(8,128)(2,1)S(1)}, bf16[128,1280]{1,0:T(8,128)(2,1)}, u32[]{:S(2)}) copy-start(bf16[128,1280]{1,0:T(8,128)(2,1)} %param.6) | copy-start | bytes 983044
  24.0 41.9 %all-to-all-start.2 = ((f32[32,16,320]{2,1,0:T(8,128)}), f32[32,16,320]{2,1,0:T(8,128)S(1)}, u32[]{:S(2)}, u32[]{:S(2)}) async-start(f32[32,16,320]{2,1,0:T(8,128)} %reshape.44), calls=%async_computation.2 | async-start | bytes 1572864 | tf_op jit(solution)/shard_map/all_to_all | solution.py:56
  65.9 25.2 %all-to-all-start = ((f32[32,16,320]{2,1,0:T(8,128)}), f32[32,16,320]{2,1,0:T(8,128)}, u32[]{:S(2)}, u32[]{:S(2)}) async-start(f32[32,16,320]{2,1,0:T(8,128)} %reshape.42), calls=%async_computation | async-start | bytes 1572864 | tf_op jit(solution)/shard_map/all_to_all | solution.py:63
  91.2 72.9 %all-to-all-start.3 = ((f32[32,16,320]{2,0,1:T(8,128)}), f32[32,16,320]{2,0,1:T(8,128)S(1)}, u32[]{:S(2)}, u32[]{:S(2)}) async-start(f32[32,16,320]{2,0,1:T(8,128)} %copy.29), calls=%async_computation.3 | async-start | bytes 1572864 | tf_op jit(solution)/shard_map/all_to_all | solution.py:55
  164.0 44.4 %all-to-all-start.1 = ((f32[32,16,320]{2,0,1:T(8,128)}), f32[32,16,320]{2,0,1:T(8,128)S(1)}, u32[]{:S(2)}, u32[]{:S(2)}) async-start(f32[32,16,320]{2,0,1:T(8,128)} %copy.27), calls=%async_computation.1 | async-start | bytes 1572864 | tf_op jit(solution)/shard_map/all_to_all | solution.py:62
  173.3 37.2 %collective-permute-start.4 = (bf16[256,320]{1,0:T(8,128)(2,1)S(1)}, bf16[256,320]{1,0:T(8,128)(2,1)S(1)}, u32[]{:S(2)}, u32[]{:S(2)}) collective-permute-start(bf16[256,320]{1,0:T(8,128)(2,1)S(1)} %bitcast.51), channel_id=1, source_target_pairs={{0,1},{1,0},{2,3},{3,2},{4,5},{5,4},{6,7},{7,6},{8,9},{9,8},{10,11... | collective-permute-start | bytes 491528 | tf_op jit(solution)/shard_map/ppermute | solution.py:17
  208.6 7.6 collective-permute-start.2
  210.8 13.1 %collective-permute-start.5 = (bf16[256,640]{1,0:T(8,128)(2,1)S(1)}, bf16[256,640]{1,0:T(8,128)(2,1)S(1)}, u32[]{:S(2)}, u32[]{:S(2)}) collective-permute-start(bf16[256,640]{1,0:T(8,128)(2,1)S(1)} %maximum_select_fusion.6), channel_id=1, source_target_pairs={{0,2},{2,0},{1,3},{3,1},{4,6},{6,4},{5,7},{7,5},{8,10},{10,8},{9,1... | collective-permute-start | bytes 983048 | tf_op jit(solution)/shard_map/ppermute | solution.py:17
  216.5 14.5 %collective-permute-start.3 = (bf16[256,640]{1,0:T(8,128)(2,1)S(1)}, bf16[256,640]{1,0:T(8,128)(2,1)}, u32[]{:S(2)}, u32[]{:S(2)}) collective-permute-start(bf16[256,640]{1,0:T(8,128)(2,1)S(1)} %maximum_select_fusion.5), channel_id=1, source_target_pairs={{0,2},{2,0},{1,3},{3,1},{4,6},{6,4},{5,7},{7,5},{8,10},{10,8},{9,1... | collective-permute-start | bytes 983048 | tf_op jit(solution)/shard_map/ppermute | solution.py:17
  234.2 1.1 copy-start.1
  234.2 4.1 copy-start.5
  235.3 17.1 %collective-permute-start.6 = (f32[256,640]{1,0:T(8,128)S(1)}, f32[256,640]{1,0:T(8,128)S(1)}, u32[]{:S(2)}, u32[]{:S(2)}) collective-permute-start(f32[256,640]{1,0:T(8,128)S(1)} %slice_select_fusion.1), channel_id=1, source_target_pairs={{0,2},{2,0},{1,3},{3,1},{4,6},{6,4},{5,7},{7,5},{8,10},{10,8},{9,1... | collective-permute-start | bytes 1966088 | tf_op jit(solution)/shard_map/ppermute | solution.py:17
  238.3 14.0 %copy-start.2 = (f32[256,1280]{1,0:T(8,128)S(1)}, f32[256,1280]{1,0:T(8,128)}, u32[]{:S(2)}) copy-start(f32[256,1280]{1,0:T(8,128)} %copy-done.1) | copy-start | bytes 3932164
  252.6 7.8 collective-permute-start.7
  257.4 18.6 %collective-permute-start.8 = (f32[256,640]{1,0:T(8,128)}, f32[256,640]{1,0:T(8,128)}, u32[]{:S(2)}, u32[]{:S(2)}) collective-permute-start(f32[256,640]{1,0:T(8,128)} %slice_select_fusion), channel_id=1, source_target_pairs={{0,2},{2,0},{1,3},{3,1},{4,6},{6,4},{5,7},{7,5},{8,10},{10,8},{9,1... | collective-permute-start | bytes 1966088 | tf_op jit(solution)/shard_map/ppermute | solution.py:17
  261.9 29.7 %all-to-all-start.4 = ((bf16[32,16,320]{2,1,0:T(8,128)(2,1)}), bf16[32,16,320]{2,1,0:T(8,128)(2,1)S(1)}, u32[]{:S(2)}, u32[]{:S(2)}) async-start(bf16[32,16,320]{2,1,0:T(8,128)(2,1)} %reshape.46), calls=%async_computation.4 | async-start | bytes 786432 | tf_op jit(solution)/shard_map/all_to_all | solution.py:129
  277.3 4.4 collective-permute-start.9
  291.6 22.2 %all-to-all-start.6 = ((bf16[32,16,320]{2,1,0:T(8,128)(2,1)}), bf16[32,16,320]{2,1,0:T(8,128)(2,1)S(1)}, u32[]{:S(2)}, u32[]{:S(2)}) async-start(bf16[32,16,320]{2,1,0:T(8,128)(2,1)} %reshape.48), calls=%async_computation.6 | async-start | bytes 786432 | tf_op jit(solution)/shard_map/all_to_all | solution.py:122
  313.8 48.4 %all-to-all-start.5 = ((bf16[32,16,320]{2,0,1:T(8,128)(2,1)}), bf16[32,16,320]{2,0,1:T(8,128)(2,1)S(1)}, u32[]{:S(2)}, u32[]{:S(2)}) async-start(bf16[32,16,320]{2,0,1:T(8,128)(2,1)} %copy.31), calls=%async_computation.5 | async-start | bytes 786432 | tf_op jit(solution)/shard_map/all_to_all | solution.py:128
  341.4 27.5 %copy-start.3 = (bf16[128,1280]{1,0:T(8,128)(2,1)S(1)}, bf16[128,1280]{1,0:T(8,128)(2,1)}, u32[]{:S(2)}) copy-start(bf16[128,1280]{1,0:T(8,128)(2,1)} %param.5) | copy-start | bytes 983044
  362.2 27.8 %all-to-all-start.7 = ((bf16[32,16,320]{2,0,1:T(8,128)(2,1)}), bf16[32,16,320]{2,0,1:T(8,128)(2,1)S(1)}, u32[]{:S(2)}, u32[]{:S(2)}) async-start(bf16[32,16,320]{2,0,1:T(8,128)(2,1)} %copy.33), calls=%async_computation.7 | async-start | bytes 786432 | tf_op jit(solution)/shard_map/all_to_all | solution.py:121
  368.4 566.3 %all-reduce.4.cloned.1.call-start = ((), (), s32[]{:S(2)}) async-start(), calls=%async_computation.8 | async-start | bytes 1310720
  390.5 9.5 copy-start.4
  391.9 3.0 collective-permute-start.10
Sparse Core Ops, SparseCore 0:
  396.3 538.3 all-reduce.3
where the time goes:
time: 1050 us; the launch traced here: 1040 us
  waiting for transfers between devices  740 us (70%)
  starting transfers between devices  153 us (15%)
  blocking collectives  102 us (10%)
  local copies, waits for them, and re-layouts  16.3 us (2%)
  between operations  15.8 us (2%)
  matrix products  14.2 us (1%)
    unnamed x2, waiting for transfers between devices  533 us
    unnamed x1, blocking collectives  102 us
    all_to_all x1, starting transfers between devices, shards(): lax.all_to_all(lax.all_to_all(in_blocks, 'dp', split_axis=0, concat_axis=...  37.6 us
    ppermute x11, starting transfers between devices, from_partner(): return lax.ppermute(block, axis, route)  37.2 us
    all_to_all x1, waiting for transfers between devices, shards(): lax.all_to_all(lax.all_to_all(grad_blocks, 'dp', split_axis=0, concat_axi...  33.1 us
    all_to_all x1, waiting for transfers between devices, shards(): lax.all_to_all(lax.all_to_all(in_blocks, 'dp', split_axis=0, concat_axis=...  33 us
    ppermute x11, waiting for transfers between devices, from_partner(): return lax.ppermute(block, axis, route)  29.5 us
    all_to_all x1, starting transfers between devices, shards(): lax.all_to_all(lax.all_to_all(spread(back_part), 'dp', split_axis=0, conc...  26.8 us
  transfers between devices with their start and end apart: 20, of which 17 were waited for; matrix products, arithmetic and copies ran while one was open for 2% of the time, Pallas kernels for 0%

commit v1 on v0

--- a/solution.py
+++ b/solution.py
@@ -147,15 +147,24 @@
         jnp.dot(dispatch_b, slot_in_grad, preferred_element_type=jnp.float32)
         + jnp.einsum("te,de->td", logit_grad, slot_param, preferred_element_type=jnp.float32)
     ).astype(jnp.bfloat16)
-    param_rows = lax.psum_scatter(
-        jnp.einsum("td,te->de", tokens, logit_grad, preferred_element_type=jnp.float32),
-        "dp",
-        scatter_dimension=0,
-        tiled=True,
+    param_part = jnp.einsum("td,te->de", tokens, logit_grad, preferred_element_type=jnp.float32)
+    param_rows = jnp.sum(
+        lax.all_to_all(
+            param_part.reshape(ranks, width // ranks, experts),
+            "dp",
+            split_axis=0,
+            concat_axis=0,
+            tiled=True,
+        ),
+        axis=0,
     )
-    param_grad = lax.psum_scatter(param_rows, "expert", scatter_dimension=1, tiled=True).astype(
-        jnp.bfloat16
-    )
+    param_cols = param_rows.reshape(width // ranks, ranks_ex, experts // ranks_ex)
+    param_grad = jnp.sum(
+        lax.all_to_all(
+            param_cols.transpose(1, 0, 2), "expert", split_axis=0, concat_axis=0, tiled=True
+        ),
+        axis=0,
+    ).astype(jnp.bfloat16)
     return (token_grad, param_grad)
 
 

time: 1050 us -> 457 us (0.44)
  waiting for transfers between devices: 740 us -> 241 us
  blocking collectives: 102 us -> 0 us
  starting transfers between devices: 153 us -> 179 us
  between operations: 15.8 us -> 1.12 us
    unnamed x2 -> x0, waiting for transfers between devices: 533 us -> none
    unnamed x1 -> x0, blocking collectives: 102 us -> none
    all_to_all x0 -> x2, waiting for transfers between devices: none -> 34.2 us  [the longest x1 25.4 us: shards(): lax.all_to_all(param_part.reshape(ranks, width // ranks, experts), 'dp',...]
    all_to_all x0 -> x2, starting transfers between devices: none -> 26.3 us  [the longest x1 21.7 us: shards(): lax.all_to_all(param_cols.transpose(1, 0, 2), 'expert', split_axis=0, con...]
  transfers between devices with their start and end apart: 20 -> 21, of which waited for: 17 -> 18; matrix products, arithmetic and copies ran while one was open for 2% -> 4% of each run, Pallas kernels for 0% -> 0%
where the time goes in v1:
time: 457 us; the launch traced here: 455 us
  waiting for transfers between devices  241 us (53%)
  starting transfers between devices  179 us (39%)
  local copies, waits for them, and re-layouts  14.8 us (3%)
  matrix products  13.3 us (3%)
  other arithmetic  6.11 us (1%)
    all_to_all x1, starting transfers between devices, shards(): lax.all_to_all(lax.all_to_all(in_blocks, 'dp', split_axis=0, concat_axis=...  37.6 us
    ppermute x11, starting transfers between devices, from_partner(): return lax.ppermute(block, axis, route)  37.2 us
    all_to_all x1, waiting for transfers between devices, shards(): lax.all_to_all(lax.all_to_all(grad_blocks, 'dp', split_axis=0, concat_axi...  33.1 us
    all_to_all x1, waiting for transfers between devices, shards(): lax.all_to_all(lax.all_to_all(in_blocks, 'dp', split_axis=0, concat_axis=...  33 us
    ppermute x11, waiting for transfers between devices, from_partner(): return lax.ppermute(block, axis, route)  29.4 us
    all_to_all x1, starting transfers between devices, shards(): lax.all_to_all(lax.all_to_all(spread(back_part), 'dp', split_axis=0, conc...  26.7 us
    all_to_all x1, waiting for transfers between devices, shards(): lax.all_to_all(param_part.reshape(ranks, width // ranks, experts), 'dp',...  25.4 us
    all_to_all x1, waiting for transfers between devices, shards(): lax.all_to_all(in_blocks, 'dp', split_axis=0, concat_axis=0, tiled=True)  25.4 us
  transfers between devices with their start and end apart: 21, of which 18 were waited for; matrix products, arithmetic and copies ran while one was open for 4% of the time, Pallas kernels for 0%

profile of v1, /device:TPU:1, one launch (start us, length us, event | category | flops | bytes accessed | tf_op | source)
XLA Modules:
  0.0 455.5 jit_solution(13581223350342270619)
XLA Ops:
  0.6 1.5 fusion.84
  2.1 8.8 %collective-permute-start = (f32[128]{0:T(128)S(1)}, f32[128]{0:T(128)S(1)}, u32[]{:S(2)}, u32[]{:S(2)}) collective-permute-start(f32[128]{0:T(128)S(1)} %get-tuple-element.7), channel_id=1, source_target_pairs={{0,1},{1,0},{2,3},{3,2},{4,5},{5,4},{6,7},{7,6},{8,9},{9,8},{10,11... | collective-permute-start | bytes 1544 | tf_op jit(solution)/shard_map/ppermute | solution.py:17
  11.9 2.2 collective-permute-start.1
  14.9 1.3 fusion.67
  16.2 1.3 reshape.50
  17.5 14.9 %all-to-all-start.2 = ((f32[32,16,320]{2,1,0:T(8,128)}), f32[32,16,320]{2,1,0:T(8,128)S(1)}, u32[]{:S(2)}, u32[]{:S(2)}) async-start(f32[32,16,320]{2,1,0:T(8,128)} %reshape.50), calls=%async_computation.2 | async-start | bytes 1572864 | tf_op jit(solution)/shard_map/all_to_all | solution.py:56
  32.8 1.3 reshape.48
  34.0 25.4 %all-to-all-done.2 = f32[32,16,320]{2,1,0:T(8,128)S(1)} async-done(((f32[32,16,320]{2,1,0:T(8,128)}), f32[32,16,320]{2,1,0:T(8,128)S(1)}, u32[]{:S(2)}, u32[]{:S(2)}) %all-to-all-start.2) | async-done | bytes 655392 | tf_op jit(solution)/shard_map/all_to_all | solution.py:56
  59.4 4.6 %all-to-all-start = ((f32[32,16,320]{2,1,0:T(8,128)}), f32[32,16,320]{2,1,0:T(8,128)}, u32[]{:S(2)}, u32[]{:S(2)}) async-start(f32[32,16,320]{2,1,0:T(8,128)} %reshape.48), calls=%async_computation | async-start | bytes 1572864 | tf_op jit(solution)/shard_map/all_to_all | solution.py:63
  64.1 1.1 copy.37
  65.2 19.4 %all-to-all-done = f32[32,16,320]{2,1,0:T(8,128)} async-done(((f32[32,16,320]{2,1,0:T(8,128)}), f32[32,16,320]{2,1,0:T(8,128)}, u32[]{:S(2)}, u32[]{:S(2)}) %all-to-all-start) | async-done | bytes 655392 | tf_op jit(solution)/shard_map/all_to_all | solution.py:63
  84.6 37.6 %all-to-all-start.3 = ((f32[32,16,320]{2,0,1:T(8,128)}), f32[32,16,320]{2,0,1:T(8,128)S(1)}, u32[]{:S(2)}, u32[]{:S(2)}) async-start(f32[32,16,320]{2,0,1:T(8,128)} %copy.37), calls=%async_computation.3 | async-start | bytes 1572864 | tf_op jit(solution)/shard_map/all_to_all | solution.py:55
  122.2 2.3 copy.35
  124.5 33.0 %all-to-all-done.3 = f32[32,16,320]{2,0,1:T(8,128)S(1)} async-done(((f32[32,16,320]{2,0,1:T(8,128)}), f32[32,16,320]{2,0,1:T(8,128)S(1)}, u32[]{:S(2)}, u32[]{:S(2)}) %all-to-all-start.3) | async-done | bytes 655392 | tf_op jit(solution)/shard_map/all_to_all | solution.py:55
  157.5 9.1 %all-to-all-start.1 = ((f32[32,16,320]{2,0,1:T(8,128)}), f32[32,16,320]{2,0,1:T(8,128)S(1)}, u32[]{:S(2)}, u32[]{:S(2)}) async-start(f32[32,16,320]{2,0,1:T(8,128)} %copy.35), calls=%async_computation.1 | async-start | bytes 1572864 | tf_op jit(solution)/shard_map/all_to_all | solution.py:62
  166.8 2.0 collective-permute-start.4
  168.8 33.1 %all-to-all-done.1 = f32[32,16,320]{2,0,1:T(8,128)S(1)} async-done(((f32[32,16,320]{2,0,1:T(8,128)}), f32[32,16,320]{2,0,1:T(8,128)S(1)}, u32[]{:S(2)}, u32[]{:S(2)}) %all-to-all-start.1) | async-done | bytes 655392 | tf_op jit(solution)/shard_map/all_to_all | solution.py:62
  202.1 1.9 collective-permute-start.2
  204.2 5.5 %collective-permute-start.5 = (bf16[256,640]{1,0:T(8,128)(2,1)S(1)}, bf16[256,640]{1,0:T(8,128)(2,1)S(1)}, u32[]{:S(2)}, u32[]{:S(2)}) collective-permute-start(bf16[256,640]{1,0:T(8,128)(2,1)S(1)} %maximum_select_fusion.6), channel_id=1, source_target_pairs={{0,2},{2,0},{1,3},{3,1},{4,6},{6,4},{5,7},{7,5},{8,10},{10,8},{9,1... | collective-permute-start | bytes 983048 | tf_op jit(solution)/shard_map/ppermute | solution.py:17
  210.0 1.9 collective-permute-start.3
  211.9 5.4 %collective-permute-done.5 = bf16[256,640]{1,0:T(8,128)(2,1)S(1)} collective-permute-done((bf16[256,640]{1,0:T(8,128)(2,1)S(1)}, bf16[256,640]{1,0:T(8,128)(2,1)S(1)}, u32[]{:S(2)}, u32[]{:S(2)}) %collective-permute-start.5) | collective-permute-done | bytes 327712 | tf_op jit(solution)/shard_map/ppermute | solution.py:17
  217.3 3.0 fusion.3
  220.4 4.1 collective-permute-done.3
  224.5 3.2 fusion.1
  228.7 3.0 collective-permute-start.6
  232.6 13.3 %collective-permute-done.6 = f32[256,640]{1,0:T(8,128)S(1)} collective-permute-done((f32[256,640]{1,0:T(8,128)S(1)}, f32[256,640]{1,0:T(8,128)S(1)}, u32[]{:S(2)}, u32[]{:S(2)}) %collective-permute-start.6) | collective-permute-done | bytes 655392 | tf_op jit(solution)/shard_map/ppermute | solution.py:17
  246.1 3.9 collective-permute-start.7
  250.9 3.0 collective-permute-start.8
  254.3 1.1 reshape.52
  255.4 11.4 %all-to-all-start.4 = ((bf16[32,16,320]{2,1,0:T(8,128)(2,1)}), bf16[32,16,320]{2,1,0:T(8,128)(2,1)S(1)}, u32[]{:S(2)}, u32[]{:S(2)}) async-start(bf16[32,16,320]{2,1,0:T(8,128)(2,1)} %reshape.52), calls=%async_computation.4 | async-start | bytes 786432 | tf_op jit(solution)/shard_map/all_to_all | solution.py:129
  266.8 2.7 collective-permute-done.8
  269.4 1.2 select_add_fusion
  270.8 3.1 collective-permute-start.9
  273.9 1.3 collective-permute-done.9
  276.7 8.4 %all-to-all-done.4 = bf16[32,16,320]{2,1,0:T(8,128)(2,1)S(1)} async-done(((bf16[32,16,320]{2,1,0:T(8,128)(2,1)}), bf16[32,16,320]{2,1,0:T(8,128)(2,1)S(1)}, u32[]{:S(2)}, u32[]{:S(2)}) %all-to-all-start.4) | async-done | bytes 327712 | tf_op jit(solution)/shard_map/all_to_all | solution.py:129
  285.1 5.0 %all-to-all-start.6 = ((bf16[32,16,320]{2,1,0:T(8,128)(2,1)}), bf16[32,16,320]{2,1,0:T(8,128)(2,1)S(1)}, u32[]{:S(2)}, u32[]{:S(2)}) async-start(bf16[32,16,320]{2,1,0:T(8,128)(2,1)} %reshape.54), calls=%async_computation.6 | async-start | bytes 786432 | tf_op jit(solution)/shard_map/all_to_all | solution.py:122
  291.0 16.3 %all-to-all-done.6 = bf16[32,16,320]{2,1,0:T(8,128)(2,1)S(1)} async-done(((bf16[32,16,320]{2,1,0:T(8,128)(2,1)}), bf16[32,16,320]{2,1,0:T(8,128)(2,1)S(1)}, u32[]{:S(2)}, u32[]{:S(2)}) %all-to-all-start.6) | async-done | bytes 327712 | tf_op jit(solution)/shard_map/all_to_all | solution.py:122
  307.3 26.7 %all-to-all-start.5 = ((bf16[32,16,320]{2,0,1:T(8,128)(2,1)}), bf16[32,16,320]{2,0,1:T(8,128)(2,1)S(1)}, u32[]{:S(2)}, u32[]{:S(2)}) async-start(bf16[32,16,320]{2,0,1:T(8,128)(2,1)} %copy.39), calls=%async_computation.5 | async-start | bytes 786432 | tf_op jit(solution)/shard_map/all_to_all | solution.py:128
  334.9 20.8 %all-to-all-done.5 = bf16[32,16,320]{2,0,1:T(8,128)(2,1)S(1)} async-done(((bf16[32,16,320]{2,0,1:T(8,128)(2,1)}), bf16[32,16,320]{2,0,1:T(8,128)(2,1)S(1)}, u32[]{:S(2)}, u32[]{:S(2)}) %all-to-all-start.5) | async-done | bytes 327712 | tf_op jit(solution)/shard_map/all_to_all | solution.py:128
  355.6 6.2 %all-to-all-start.7 = ((bf16[32,16,320]{2,0,1:T(8,128)(2,1)}), bf16[32,16,320]{2,0,1:T(8,128)(2,1)S(1)}, u32[]{:S(2)}, u32[]{:S(2)}) async-start(bf16[32,16,320]{2,0,1:T(8,128)(2,1)} %copy.41), calls=%async_computation.7 | async-start | bytes 786432 | tf_op jit(solution)/shard_map/all_to_all | solution.py:121
  362.6 20.8 %all-to-all-done.7 = bf16[32,16,320]{2,0,1:T(8,128)(2,1)S(1)} async-done(((bf16[32,16,320]{2,0,1:T(8,128)(2,1)}), bf16[32,16,320]{2,0,1:T(8,128)(2,1)S(1)}, u32[]{:S(2)}, u32[]{:S(2)}) %all-to-all-start.7) | async-done | bytes 327712 | tf_op jit(solution)/shard_map/all_to_all | solution.py:121
  383.9 1.3 multiply_reduce_fusion.1
  385.2 1.9 collective-permute-start.10
  389.7 4.6 %all-to-all-start.8 = ((f32[32,40,128]{2,1,0:T(8,128)}), f32[32,40,128]{2,1,0:T(8,128)}, u32[]{:S(2)}, u32[]{:S(2)}) async-start(f32[32,40,128]{2,1,0:T(8,128)} %bitcast.11), calls=%async_computation.8 | async-start | bytes 1310720 | tf_op jit(solution)/shard_map/all_to_all | solution.py:152
  394.7 25.4 %all-to-all-done.8 = f32[32,40,128]{2,1,0:T(8,128)} async-done(((f32[32,40,128]{2,1,0:T(8,128)}), f32[32,40,128]{2,1,0:T(8,128)}, u32[]{:S(2)}, u32[]{:S(2)}) %all-to-all-start.8) | async-done | bytes 655392 | tf_op jit(solution)/shard_map/all_to_all | solution.py:152
  420.1 1.1 reduce_sum.78
  422.1 21.7 %all-to-all-start.9 = ((f32[16,1,320]{2,1,0:T(1,128)}), f32[16,1,320]{2,1,0:T(1,128)S(1)}, u32[]{:S(2)}, u32[]{:S(2)}) async-start(f32[16,1,320]{2,1,0:T(1,128)} %reshape.58), calls=%async_computation.9 | async-start | bytes 49152 | tf_op jit(solution)/shard_map/all_to_all | solution.py:163
  444.7 8.8 %all-to-all-done.9 = f32[16,1,320]{2,1,0:T(1,128)S(1)} async-done(((f32[16,1,320]{2,1,0:T(1,128)}), f32[16,1,320]{2,1,0:T(1,128)S(1)}, u32[]{:S(2)}, u32[]{:S(2)}) %all-to-all-start.9) | async-done | bytes 20512 | tf_op jit(solution)/shard_map/all_to_all | solution.py:163
  (60 shorter events, 17.2 us)
Async XLA Ops:
  0.6 223.8 %copy-start = (bf16[1,640,1280]{2,1,0:T(8,128)(2,1)S(1)}, bf16[1,640,1280]{2,1,0:T(8,128)(2,1)}, u32[]{:S(2)}) copy-start(bf16[1,640,1280]{2,1,0:T(8,128)(2,1)} %param.9) | copy-start | bytes 4915204
  2.1 9.6 %collective-permute-start = (f32[128]{0:T(128)S(1)}, f32[128]{0:T(128)S(1)}, u32[]{:S(2)}, u32[]{:S(2)}) collective-permute-start(f32[128]{0:T(128)S(1)} %get-tuple-element.7), channel_id=1, source_target_pairs={{0,1},{1,0},{2,3},{3,2},{4,5},{5,4},{6,7},{7,6},{8,9},{9,8},{10,11... | collective-permute-start | bytes 1544 | tf_op jit(solution)/shard_map/ppermute | solution.py:17
  11.9 3.0 collective-permute-start.1
  16.2 16.2 %copy-start.6 = (bf16[128,1280]{1,0:T(8,128)(2,1)S(1)}, bf16[128,1280]{1,0:T(8,128)(2,1)}, u32[]{:S(2)}) copy-start(bf16[128,1280]{1,0:T(8,128)(2,1)} %param.6) | copy-start | bytes 983044
  17.5 41.9 %all-to-all-start.2 = ((f32[32,16,320]{2,1,0:T(8,128)}), f32[32,16,320]{2,1,0:T(8,128)S(1)}, u32[]{:S(2)}, u32[]{:S(2)}) async-start(f32[32,16,320]{2,1,0:T(8,128)} %reshape.50), calls=%async_computation.2 | async-start | bytes 1572864 | tf_op jit(solution)/shard_map/all_to_all | solution.py:56
  59.4 25.2 %all-to-all-start = ((f32[32,16,320]{2,1,0:T(8,128)}), f32[32,16,320]{2,1,0:T(8,128)}, u32[]{:S(2)}, u32[]{:S(2)}) async-start(f32[32,16,320]{2,1,0:T(8,128)} %reshape.48), calls=%async_computation | async-start | bytes 1572864 | tf_op jit(solution)/shard_map/all_to_all | solution.py:63
  84.6 72.9 %all-to-all-start.3 = ((f32[32,16,320]{2,0,1:T(8,128)}), f32[32,16,320]{2,0,1:T(8,128)S(1)}, u32[]{:S(2)}, u32[]{:S(2)}) async-start(f32[32,16,320]{2,0,1:T(8,128)} %copy.37), calls=%async_computation.3 | async-start | bytes 1572864 | tf_op jit(solution)/shard_map/all_to_all | solution.py:55
  157.5 44.4 %all-to-all-start.1 = ((f32[32,16,320]{2,0,1:T(8,128)}), f32[32,16,320]{2,0,1:T(8,128)S(1)}, u32[]{:S(2)}, u32[]{:S(2)}) async-start(f32[32,16,320]{2,0,1:T(8,128)} %copy.35), calls=%async_computation.1 | async-start | bytes 1572864 | tf_op jit(solution)/shard_map/all_to_all | solution.py:62
  166.8 37.2 %collective-permute-start.4 = (bf16[256,320]{1,0:T(8,128)(2,1)S(1)}, bf16[256,320]{1,0:T(8,128)(2,1)S(1)}, u32[]{:S(2)}, u32[]{:S(2)}) collective-permute-start(bf16[256,320]{1,0:T(8,128)(2,1)S(1)} %bitcast.56), channel_id=1, source_target_pairs={{0,1},{1,0},{2,3},{3,2},{4,5},{5,4},{6,7},{7,6},{8,9},{9,8},{10,11... | collective-permute-start | bytes 491528 | tf_op jit(solution)/shard_map/ppermute | solution.py:17
  202.1 7.6 %collective-permute-start.2 = (bf16[256,320]{1,0:T(8,128)(2,1)S(1)}, bf16[256,320]{1,0:T(8,128)(2,1)S(1)}, u32[]{:S(2)}, u32[]{:S(2)}) collective-permute-start(bf16[256,320]{1,0:T(8,128)(2,1)S(1)} %bitcast.58), channel_id=1, source_target_pairs={{0,1},{1,0},{2,3},{3,2},{4,5},{5,4},{6,7},{7,6},{8,9},{9,8},{10,11... | collective-permute-start | bytes 491528 | tf_op jit(solution)/shard_map/ppermute | solution.py:17
  204.2 13.1 %collective-permute-start.5 = (bf16[256,640]{1,0:T(8,128)(2,1)S(1)}, bf16[256,640]{1,0:T(8,128)(2,1)S(1)}, u32[]{:S(2)}, u32[]{:S(2)}) collective-permute-start(bf16[256,640]{1,0:T(8,128)(2,1)S(1)} %maximum_select_fusion.6), channel_id=1, source_target_pairs={{0,2},{2,0},{1,3},{3,1},{4,6},{6,4},{5,7},{7,5},{8,10},{10,8},{9,1... | collective-permute-start | bytes 983048 | tf_op jit(solution)/shard_map/ppermute | solution.py:17
  210.0 14.5 %collective-permute-start.3 = (bf16[256,640]{1,0:T(8,128)(2,1)S(1)}, bf16[256,640]{1,0:T(8,128)(2,1)}, u32[]{:S(2)}, u32[]{:S(2)}) collective-permute-start(bf16[256,640]{1,0:T(8,128)(2,1)S(1)} %maximum_select_fusion.5), channel_id=1, source_target_pairs={{0,2},{2,0},{1,3},{3,1},{4,6},{6,4},{5,7},{7,5},{8,10},{10,8},{9,1... | collective-permute-start | bytes 983048 | tf_op jit(solution)/shard_map/ppermute | solution.py:17
  227.7 1.1 copy-start.1
  227.7 4.1 copy-start.5
  228.7 17.1 %collective-permute-start.6 = (f32[256,640]{1,0:T(8,128)S(1)}, f32[256,640]{1,0:T(8,128)S(1)}, u32[]{:S(2)}, u32[]{:S(2)}) collective-permute-start(f32[256,640]{1,0:T(8,128)S(1)} %slice_select_fusion.1), channel_id=1, source_target_pairs={{0,2},{2,0},{1,3},{3,1},{4,6},{6,4},{5,7},{7,5},{8,10},{10,8},{9,1... | collective-permute-start | bytes 1966088 | tf_op jit(solution)/shard_map/ppermute | solution.py:17
  231.8 14.0 %copy-start.2 = (f32[256,1280]{1,0:T(8,128)S(1)}, f32[256,1280]{1,0:T(8,128)}, u32[]{:S(2)}) copy-start(f32[256,1280]{1,0:T(8,128)} %copy-done.1) | copy-start | bytes 3932164
  246.1 7.8 %collective-permute-start.7 = (f32[256,320]{1,0:T(8,128)S(1)}, f32[256,320]{1,0:T(8,128)S(1)}, u32[]{:S(2)}, u32[]{:S(2)}) collective-permute-start(f32[256,320]{1,0:T(8,128)S(1)} %slice_select_fusion.3), channel_id=1, source_target_pairs={{0,1},{1,0},{2,3},{3,2},{4,5},{5,4},{6,7},{7,6},{8,9},{9,8},{10,11... | collective-permute-start | bytes 983048 | tf_op jit(solution)/shard_map/ppermute | solution.py:17
  250.9 18.6 %collective-permute-start.8 = (f32[256,640]{1,0:T(8,128)}, f32[256,640]{1,0:T(8,128)}, u32[]{:S(2)}, u32[]{:S(2)}) collective-permute-start(f32[256,640]{1,0:T(8,128)} %slice_select_fusion), channel_id=1, source_target_pairs={{0,2},{2,0},{1,3},{3,1},{4,6},{6,4},{5,7},{7,5},{8,10},{10,8},{9,1... | collective-permute-start | bytes 1966088 | tf_op jit(solution)/shard_map/ppermute | solution.py:17
  255.4 29.7 %all-to-all-start.4 = ((bf16[32,16,320]{2,1,0:T(8,128)(2,1)}), bf16[32,16,320]{2,1,0:T(8,128)(2,1)S(1)}, u32[]{:S(2)}, u32[]{:S(2)}) async-start(bf16[32,16,320]{2,1,0:T(8,128)(2,1)} %reshape.52), calls=%async_computation.4 | async-start | bytes 786432 | tf_op jit(solution)/shard_map/all_to_all | solution.py:129
  270.8 4.4 collective-permute-start.9
  285.1 22.2 %all-to-all-start.6 = ((bf16[32,16,320]{2,1,0:T(8,128)(2,1)}), bf16[32,16,320]{2,1,0:T(8,128)(2,1)S(1)}, u32[]{:S(2)}, u32[]{:S(2)}) async-start(bf16[32,16,320]{2,1,0:T(8,128)(2,1)} %reshape.54), calls=%async_computation.6 | async-start | bytes 786432 | tf_op jit(solution)/shard_map/all_to_all | solution.py:122
  307.3 48.3 %all-to-all-start.5 = ((bf16[32,16,320]{2,0,1:T(8,128)(2,1)}), bf16[32,16,320]{2,0,1:T(8,128)(2,1)S(1)}, u32[]{:S(2)}, u32[]{:S(2)}) async-start(bf16[32,16,320]{2,0,1:T(8,128)(2,1)} %copy.39), calls=%async_computation.5 | async-start | bytes 786432 | tf_op jit(solution)/shard_map/all_to_all | solution.py:128
  334.9 27.4 %copy-start.3 = (bf16[128,1280]{1,0:T(8,128)(2,1)S(1)}, bf16[128,1280]{1,0:T(8,128)(2,1)}, u32[]{:S(2)}) copy-start(bf16[128,1280]{1,0:T(8,128)(2,1)} %param.5) | copy-start | bytes 983044
  355.6 27.8 %all-to-all-start.7 = ((bf16[32,16,320]{2,0,1:T(8,128)(2,1)}), bf16[32,16,320]{2,0,1:T(8,128)(2,1)S(1)}, u32[]{:S(2)}, u32[]{:S(2)}) async-start(bf16[32,16,320]{2,0,1:T(8,128)(2,1)} %copy.41), calls=%async_computation.7 | async-start | bytes 786432 | tf_op jit(solution)/shard_map/all_to_all | solution.py:121
  385.2 3.0 collective-permute-start.10
  388.6 5.7 %copy-start.4 = (bf16[1280,128]{1,0:T(8,128)(2,1)S(1)}, bf16[1280,128]{1,0:T(8,128)(2,1)}, u32[]{:S(2)}) copy-start(bf16[1280,128]{1,0:T(8,128)(2,1)} %param.7) | copy-start | bytes 983044
  389.7 30.3 %all-to-all-start.8 = ((f32[32,40,128]{2,1,0:T(8,128)}), f32[32,40,128]{2,1,0:T(8,128)}, u32[]{:S(2)}, u32[]{:S(2)}) async-start(f32[32,40,128]{2,1,0:T(8,128)} %bitcast.11), calls=%async_computation.8 | async-start | bytes 1310720 | tf_op jit(solution)/shard_map/all_to_all | solution.py:152
  422.1 31.5 %all-to-all-start.9 = ((f32[16,1,320]{2,1,0:T(1,128)}), f32[16,1,320]{2,1,0:T(1,128)S(1)}, u32[]{:S(2)}, u32[]{:S(2)}) async-start(f32[16,1,320]{2,1,0:T(1,128)} %reshape.58), calls=%async_computation.9 | async-start | bytes 49152 | tf_op jit(solution)/shard_map/all_to_all | solution.py:163

commit v2 on v0

v2 whole, which is shorter than its diff:
```python
import functools

import jax
import jax.numpy as jnp
from jax import lax
from jax.experimental import pallas as pl
from jax.experimental.pallas import tpu as pltpu
from jax.sharding import PartitionSpec as P

MESH = pl.DeviceIdType.MESH
PLANE_Y = 4

gelu_scale = 0.7978845608
gelu_cubic = 0.044715

F32 = jnp.float32
BF16 = jnp.bfloat16


def gelu_parts(pre_act):
    inner_arg = gelu_scale * (pre_act + gelu_cubic * pre_act * pre_act * pre_act)
    tangent = jnp.tanh(inner_arg)
    gelu_value = 0.5 * pre_act * (1.0 + tangent)
    gelu_slope = 0.5 * (1.0 + tangent) + 0.5 * pre_act * (1.0 - tangent * tangent) * gelu_scale * (
        1.0 + 3.0 * gelu_cubic * pre_act * pre_act
    )
    return (gelu_value, gelu_slope)


def dot(a, b, ca, cb):
    return lax.dot_general(a, b, (((ca,), (cb,)), ((), ())), preferred_element_type=F32)


def tiles(extent, step=256):
    return [(at, min(step, extent - at)) for at in range(0, extent, step)]


def log2(n):
    return n.bit_length() - 1


def kernel(
    nx, ny, zl_n,
    tok_hbm, og_hbm, sp_hbm, w1_hbm, w2_hbm,
    tg_ref, pg_ref,
    tok, og, sp, w1, w2, spt, tokt, disp, comb, disp_b, lg_b,
    s_buf, r_buf, t_buf, x_buf, gv, pgd, p_buf, o_send, o_recv, u_buf, v_buf, q_buf, b_buf, c_buf, g_buf,
    pg_send, pg_recv, pad, f2_send, f2_recv,
    load_sem, swap_s, swap_r, p1_s, p1_r, p2_s, p2_r, rl_s, dd_s, dd_r, o_s, o_r,
    v_s, v_r, b_s, b_r, g_s, g_r, gd_s, gd_r, f1_s, f1_r, f2_s, f2_r,
):
    plane, ring, pairs = nx * ny, 2 * zl_n, zl_n
    at_dp, at_ex = lax.axis_index("dp"), lax.axis_index("expert")
    core, zl = lax.rem(at_ex, 2), lax.div(at_ex, 2)
    y, xz = lax.rem(at_dp, ny), lax.div(at_dp, ny)
    zh, x = lax.rem(xz, 2), lax.div(xz, 2)
    z, xy = zh * zl_n + zl, x * ny + y
    sign = 2 * lax.rem(z, 2) - 1
    pair = lax.div(z, 2)
    other = 1 - core

    def turn(v):
        return lax.rem(v + 2 * ring, ring)

    def shift(j):
        return lax.rem(xy + j, plane)

    def device(xy_to, z_to, core_to):
        x_to, y_to = lax.div(xy_to, ny), lax.rem(xy_to, ny)
        return (
            (x_to * 2 + lax.div(z_to, zl_n)) * ny + y_to,
            lax.rem(z_to, zl_n) * 2 + core_to,
        )

    partner = device(xy, z, other)
    sibling_z = turn(z - sign)
    sibling = device(xy, sibling_z, core)
    started = []

    def send(src, dst, send_sem, recv_sem, to):
        copy = pltpu.make_async_remote_copy(
            src_ref=src, dst_ref=dst, send_sem=send_sem, recv_sem=recv_sem,
            device_id=to, device_id_type=MESH,
        )
        copy.start()
        started.append(copy)

    def arrived(dst, recv_sem):
        pltpu.make_async_remote_copy(
            src_ref=dst, dst_ref=dst, send_sem=recv_sem, recv_sem=recv_sem,
            device_id=partner, device_id_type=MESH,
        ).wait_recv()

    rows, width = tok_hbm.shape
    half = width // 2
    image = 2 * rows
    slots = plane * pairs
    own_cols = pl.ds(pl.multiple_of(core * half, half), half)

    barrier = pltpu.get_barrier_semaphore()
    pl.semaphore_signal(barrier, inc=1, device_id=partner, device_id_type=MESH)
    for j in range(1, plane):
        pl.semaphore_signal(barrier, inc=1, device_id=device(shift(j), z, core), device_id_type=MESH)
    for j in range(1, ring):
        for to in range(2):
            pl.semaphore_signal(
                barrier, inc=1, device_id=device(xy, turn(z + j), to), device_id_type=MESH
            )

    loads = [
        pltpu.make_async_copy(src, dst, load_sem.at[i])
        for i, (src, dst) in enumerate(
            [(tok_hbm, tok.at[core]), (og_hbm, og.at[core]), (sp_hbm, sp), (w1_hbm.at[0], w1), (w2_hbm.at[0], w2)]
        )
    ]
    for load in loads:
        load.start()

    place = lax.broadcasted_iota(jnp.int32, (slots, slots), 0)
    zl2_n = pairs // 2
    of_place = (
        (place >> log2(pairs * ny)) * (2 * ny * zl2_n)
        + ((place >> log2(zl2_n)) & 1) * (ny * zl2_n)
        + ((place >> log2(pairs)) & (ny - 1)) * zl2_n
        + (place & (zl2_n - 1))
    )
    slot_order = (lax.broadcasted_iota(jnp.int32, (slots, slots), 1) == of_place).astype(F32).astype(BF16)
    loads[2].wait()
    spt[...] = dot(slot_order, sp[...], 1, 1).astype(BF16)
    loads[0].wait()
    loads[1].wait()

    pl.semaphore_wait(barrier, plane + 2 * (ring - 1))
    send(tok.at[core], tok.at[core], swap_s.at[0], swap_r.at[0], partner)
    send(og.at[core], og.at[core], swap_s.at[1], swap_r.at[1], partner)
    arrived(tok.at[other], swap_r.at[0])

    tok_all = tok[...].reshape(image, width)
    logits = dot(spt[...], tok_all, 1, 1)
    col_exp = jnp.exp(logits - jnp.max(logits, axis=1, keepdims=True))
    dispatch = col_exp / jnp.sum(col_exp, axis=1, keepdims=True)
    row_exp = jnp.exp(logits - jnp.max(logits, axis=0, keepdims=True))
    combine = row_exp / jnp.sum(row_exp, axis=0, keepdims=True)
    disp[...] = dispatch
    comb[...] = combine
    disp_b[...] = dispatch.astype(BF16)
    slot_in = dot(dispatch.astype(BF16), tok[:, :, own_cols].reshape(image, half), 1, 0)
    arrived(og.at[other], swap_r.at[1])
    slot_grad = dot(combine.astype(BF16), og[:, :, own_cols].reshape(image, half), 1, 0)
    s_buf[...] = jnp.concatenate(
        [slot_in.reshape(plane, pairs, half), slot_grad.reshape(plane, pairs, half)], axis=1
    ).astype(BF16)

    for j in range(1, plane):
        to = shift(j)
        send(s_buf.at[to], r_buf.at[xy], p1_s.at[j], p1_r.at[xy], device(to, z, core))
    r_buf[xy] = s_buf[xy]

    cells = 2 * pairs * plane
    first_at = lax.broadcasted_iota(jnp.int32, (cells, cells), 0)
    second_at = lax.broadcasted_iota(jnp.int32, (cells, cells), 1)

    def by_source(at):
        source = at & (plane - 1)
        kind = (at >> log2(plane)) & 1
        return source * (2 * pairs) + kind * pairs + (at >> log2(2 * plane))

    to_pairs = (second_at == by_source(first_at)).astype(F32).astype(BF16)
    to_sources = (first_at == by_source(second_at)).astype(F32).astype(BF16)

    for j in range(1, plane):
        arrived(r_buf.at[shift(j)], p1_r.at[shift(j)])
    t_buf[...] = dot(to_pairs, r_buf[...].reshape(cells, half), 1, 0).astype(BF16).reshape(
        pairs, 2, plane, half
    )

    here = x_buf.at[core, :, z]
    reach = pairs - 1
    hops = [(sign, d) for d in range(1, pairs, 2)] + [(-sign, d) for d in range(2, pairs, 2)]
    hops.sort(key=lambda hop: hop[1])
    for j, (way, d) in enumerate(hops):
        to = turn(z + way * d)
        send(t_buf.at[lax.div(to, 2)], here, p2_s.at[j], p2_r.at[z], device(xy, to, core))
    send(t_buf.at[pair], here, p2_s.at[reach], p2_r.at[z], sibling)
    send(t_buf.at[pair], here, dd_s.at[z], dd_r.at[z], partner)
    x_buf[core, :, z] = t_buf[pair]

    for at, n in tiles(width, 128):
        tokt[at : at + n] = tok[:, :, at : at + n].reshape(image, n).astype(F32).T.astype(BF16)

    def take(src):
        arrived(x_buf.at[core, :, src], p2_r.at[src])
        send(x_buf.at[core, :, src], x_buf.at[core, :, src], dd_s.at[src], dd_r.at[src], partner)

    for j in range(1, reach + 1):
        src = turn(z + sign * j)
        take(src)
        slot = x_buf.at[core, :, src]
        send(slot, slot, rl_s.at[j], p2_r.at[src], sibling)
        take(turn(z - sign * j))
    take(turn(z - sign * pairs))
    for j in range(ring):
        src = turn(z + j)
        arrived(x_buf.at[other, :, src], dd_r.at[src])

    loads[3].wait()
    loads[4].wait()
    images = ring * plane
    hidden = w1.shape[0]

    def both(kind, weights, at, n):
        return sum(
            dot(x_buf[h, kind].reshape(images, half), weights[at : at + n, h * half : (h + 1) * half], 1, 1)
            for h in range(2)
        )

    for at, n in tiles(hidden):
        gelu_value, gelu_slope = gelu_parts(both(0, w1, at, n))
        gv[:, at : at + n] = gelu_value.astype(BF16)
        pgd[:, at : at + n] = (both(1, w2, at, n) * gelu_slope).astype(BF16)

    def product(kind, whose, at, n):
        left, right = ((gv, w2), (pgd, w1))[kind]
        cols = pl.ds(pl.multiple_of(whose * half + at, 128), n)
        return dot(left[...], right[:, cols], 1, 0).reshape(ring, plane, n)

    for kind in range(2):
        for at, n in tiles(half):
            o_send[kind, :, :, at : at + n] = product(kind, other, at, n).astype(BF16)
        send(o_send.at[kind], o_recv.at[kind], o_s.at[kind], o_r.at[kind], partner)
    for kind in range(2):
        for at, n in tiles(half):
            p_buf[kind, :, :, at : at + n] = product(kind, core, at, n)
    for kind in range(2):
        arrived(o_recv.at[kind], o_r.at[kind])
        p_buf[kind] = p_buf[kind] + o_recv[kind].astype(F32)
        u_buf[kind] = p_buf[kind].astype(BF16)

    for j in range(1, pairs + 1):
        to = turn(z - sign * (pairs + 1 - j))
        send(u_buf.at[:, to], v_buf.at[:, to], v_s.at[j - 1], v_r.at[to], sibling)
    for j in range(reach, 0, -1):
        to = turn(z + sign * j)
        arrived(v_buf.at[:, to], v_r.at[to])
        q_buf[j - 1] = (p_buf[:, to] + v_buf[:, to].astype(F32)).astype(BF16)
        send(q_buf.at[j - 1], b_buf.at[pair], b_s.at[j - 1], b_r.at[pair], device(xy, to, core))
    arrived(v_buf.at[:, z], v_r.at[z])
    b_buf[pair] = (p_buf[:, z] + v_buf[:, z].astype(F32)).astype(BF16)
    for j in range(1, pairs):
        src = lax.rem(pair + j, pairs)
        arrived(b_buf.at[src], b_r.at[src])
    c_buf[...] = dot(to_sources, b_buf[...].reshape(cells, half), 1, 0).astype(BF16).reshape(
        plane, 2 * pairs, half
    )

    def hand_over(src):
        slot = g_buf.at[core, src]
        send(slot, slot, gd_s.at[src], gd_r.at[src], partner)

    for j in range(1, plane):
        to = shift(j)
        send(c_buf.at[to], g_buf.at[core, xy], g_s.at[j], g_r.at[xy], device(to, z, core))
    g_buf[core, xy] = c_buf[xy]
    hand_over(xy)
    for j in range(1, plane):
        src = shift(plane - j)
        arrived(g_buf.at[core, src], g_r.at[src])
        hand_over(src)
    for j in range(plane):
        src = shift(j)
        arrived(g_buf.at[other, src], gd_r.at[src])

    halves = [g_buf[h].astype(F32) for h in range(2)]
    slot_out = [g[:, :pairs].reshape(slots, half).astype(BF16) for g in halves]
    slot_in_grad = [g[:, pairs:].reshape(slots, half).astype(BF16) for g in halves]

    def inner(values, against):
        return sum(
            dot(values[h], against[:, :, h * half : (h + 1) * half].reshape(image, half), 1, 1)
            for h in range(2)
        )

    comb_grad = inner(slot_out, og)
    disp_grad = inner(slot_in_grad, tok)
    combine, dispatch = comb[...], disp[...]
    comb_inner = jnp.sum(combine * comb_grad, axis=0, keepdims=True)
    disp_inner = jnp.sum(dispatch * disp_grad, axis=1, keepdims=True)
    logit_grad = combine * (comb_grad - comb_inner) + dispatch * (disp_grad - disp_inner)
    lg_b[...] = logit_grad.astype(BF16)

    in_order = dot(lg_b[...], slot_order, 0, 0).astype(BF16)
    block = width // (2 * plane)
    for x_to in range(nx):
        strip = pl.ds(pl.multiple_of(x_to * 2 * ny * block + core * ny * block, 16), ny * block)
        pg_send[x_to * ny : (x_to + 1) * ny] = dot(tokt[strip, :], in_order, 1, 0).reshape(ny, block, slots)
    for j in range(1, plane):
        to = shift(j)
        send(pg_send.at[to], pg_recv.at[xy], f1_s.at[j], f1_r.at[xy], device(to, z, core))

    own_rows = pl.ds(pl.multiple_of(core * rows, rows), rows)
    for h in range(2):
        cols = slice(h * half, (h + 1) * half)
        tg_ref[:, cols] = (
            dot(disp_b[:, own_rows], slot_in_grad[h], 0, 0) + dot(lg_b[:, own_rows], spt[:, cols], 0, 0)
        ).astype(BF16)

    total = pg_send[xy]
    for j in range(1, plane):
        src = shift(plane - j)
        arrived(pg_recv.at[src], f1_r.at[src])
        total = total + pg_recv[src]
    pad[...] = jnp.zeros_like(pad)
    pad[:block, :slots] = total
    per = slots // ring
    f2_send[...] = pad[...].T[:slots].reshape(ring, per, pad.shape[0])

    for j in range(1, ring):
        to = turn(at_ex + j)
        send(
            f2_send.at[to], f2_recv.at[z], f2_s.at[j], f2_r.at[z],
            device(xy, core * zl_n + lax.div(to, 2), lax.rem(to, 2)),
        )
    stays = zh == core

    def away(start):
        copy = pltpu.make_async_remote_copy(
            src_ref=f2_send.at[at_ex], dst_ref=f2_recv.at[z], send_sem=f2_s.at[0], recv_sem=f2_r.at[z],
            device_id=device(xy, core * zl_n + zl, core), device_id_type=MESH,
        )
        if start:
            copy.start()
        else:
            copy.wait_send()

    @pl.when(stays)
    def _():
        f2_recv[z] = f2_send[at_ex]

    @pl.when(jnp.logical_not(stays))
    def _():
        away(True)
        arrived(f2_recv.at[z], f2_r.at[z])

    for j in range(1, ring):
        src = turn(z + j)
        arrived(f2_recv.at[src], f2_r.at[src])
    summed = jnp.sum(f2_recv[...], axis=0)
    pad[:per] = summed
    pg_ref[...] = pad[...].T[:block, :per].astype(BF16)

    @pl.when(jnp.logical_not(stays))
    def _():
        away(False)

    for copy in started:
        copy.wait_send()


def shards(ny, tokens, out_grad, slot_param, w_in, w_out):
    dp, ex = lax.axis_size("dp"), lax.axis_size("expert")
    nx, zl_n = dp // (2 * ny), ex // 2
    plane, ring, pairs = nx * ny, 2 * zl_n, zl_n
    rows, width = tokens.shape
    slots = slot_param.shape[1]
    hidden = w_in.shape[1]
    half, image, images = width // 2, 2 * rows, ring * plane
    block, per = width // dp, slots // ex
    side = max(128, slots)
    dma = pltpu.SemaphoreType.DMA
    vmem = pltpu.VMEM
    return pl.pallas_call(
        functools.partial(kernel, nx, ny, zl_n),
        out_shape=(
            jax.ShapeDtypeStruct((rows, width), BF16),
            jax.ShapeDtypeStruct((block, per), BF16),
        ),
        in_specs=[pl.BlockSpec(memory_space=pl.ANY)] * 5,
        out_specs=(pl.BlockSpec(memory_space=pltpu.VMEM),) * 2,
        scratch_shapes=[
            vmem((2, rows, width), BF16),
            vmem((2, rows, width), BF16),
            vmem((width, slots), BF16),
            vmem((hidden, width), BF16),
            vmem((hidden, width), BF16),
            vmem((slots, width), BF16),
            vmem((width, image), BF16),
            vmem((slots, image), F32),
            vmem((slots, image), F32),
            vmem((slots, image), BF16),
            vmem((slots, image), BF16),
            vmem((plane, 2 * pairs, half), BF16),
            vmem((plane, 2 * pairs, half), BF16),
            vmem((pairs, 2, plane, half), BF16),
            vmem((2, 2, ring, plane, half), BF16),
            vmem((images, hidden), BF16),
            vmem((images, hidden), BF16),
            vmem((2, ring, plane, half), F32),
            vmem((2, ring, plane, half), BF16),
            vmem((2, ring, plane, half), BF16),
            vmem((2, ring, plane, half), BF16),
            vmem((2, ring, plane, half), BF16),
            vmem((pairs - 1, 2, plane, half), BF16),
            vmem((pairs, 2, plane, half), BF16),
            vmem((plane, 2 * pairs, half), BF16),
            vmem((2, plane, 2 * pairs, half), BF16),
            vmem((plane, block, slots), F32),
            vmem((plane, block, slots), F32),
            vmem((side, side), F32),
            vmem((ring, per, side), F32),
            vmem((ring, per, side), F32),
            dma((5,)),
            dma((2,)), dma((2,)),
            dma((plane,)), dma((plane,)),
            dma((pairs,)), dma((ring,)), dma((pairs,)),
            dma((ring,)), dma((ring,)),
            dma((2,)), dma((2,)),
            dma((pairs,)), dma((ring,)),
            dma((pairs,)), dma((pairs,)),
            dma((plane,)), dma((plane,)),
            dma((plane,)), dma((plane,)),
            dma((plane,)), dma((plane,)),
            dma((ring,)), dma((ring,)),
        ],
        compiler_params=pltpu.CompilerParams(
            collective_id=0, has_side_effects=True, vmem_limit_bytes=44 << 20
        ),
    )(tokens, out_grad, slot_param, w_in, w_out)


def solution(mesh):
    placed = (
        P(("dp", "expert"), None),
        P(("dp", "expert"), None),
        P(),
        P(("dp", "expert"), None, None),
        P(("dp", "expert"), None, None),
    )
    return jax.shard_map(
        functools.partial(shards, PLANE_Y),
        mesh=mesh,
        in_specs=placed,
        out_specs=(P(("dp", "expert"), None), P("dp", "expert")),
        check_vma=False,
    )
```

time: 1050 us -> 110 us (0.10)
  waiting for transfers between devices: 740 us -> 0 us
  starting transfers between devices: 153 us -> 0 us
  Pallas kernels: 0 us -> 102 us
  blocking collectives: 102 us -> 0 us
  between operations: 15.8 us -> 0.65 us
  matrix products: 14.2 us -> 0 us
    unnamed x2 -> x0, waiting for transfers between devices: 533 us -> none
    all_to_all x8 -> x0, waiting for transfers between devices: 177 us -> none  [the longest x1 33.1 us: shards(): lax.all_to_all(lax.all_to_all(grad_blocks, 'dp', split_axis=0, concat_axi...]
    all_to_all x8 -> x0, starting transfers between devices: 116 us -> none  [the longest x1 37.6 us: shards(): lax.all_to_all(lax.all_to_all(in_blocks, 'dp', split_axis=0, concat_axis=...]
    pallas_call x0 -> x1, Pallas kernels: none -> 102 us  [shards(): pl.pallas_call(functools.partial(kernel, nx, ny, zl_n), out_shape=(jax.Sh...]
    unnamed x1 -> x0, blocking collectives: 102 us -> none
    ppermute x11 -> x0, starting transfers between devices: 37.2 us -> none  [from_partner(): return lax.ppermute(block, axis, route)]
    ppermute x11 -> x0, waiting for transfers between devices: 29.5 us -> none  [from_partner(): return lax.ppermute(block, axis, route)]
    dot_general x11 -> x0, matrix products: 14.2 us -> none  [the longest x1 3.19 us: shards(): back_part = jnp.dot(pre_grad, first, preferred_element_type=jnp.float32)]
  transfers between devices with their start and end apart: 20 -> 0, of which waited for: 17 -> 0; matrix products, arithmetic and copies ran while one was open for 2% -> 0% of each run, Pallas kernels for 0% -> 0%
where the time goes in v2:
time: 110 us
  Pallas kernels  102 us (93%)
  local copies, waits for them, and re-layouts  7.15 us (6%)
    pallas_call x1, Pallas kernels, shards(): pl.pallas_call(functools.partial(kernel, nx, ny, zl_n), out_shape=(jax.Sh...  102 us
    unnamed x11, local copies, waits for them, and re-layouts  6.49 us

profile of v2, /device:TPU:1, one launch (start us, length us, event | category | flops | bytes accessed | tf_op | source)
XLA Modules:
  0.0 109.5 jit_solution(13762216655937671637)
XLA Ops:
  0.6 0.0 copy-start
  0.6 1.4 %copy-done = bf16[1,640,1280]{2,1,0:T(8,128)(2,1)S(1)} copy-done((bf16[1,640,1280]{2,1,0:T(8,128)(2,1)S(1)}, bf16[1,640,1280]{2,1,0:T(8,128)(2,1)}, u32[]{:S(2)}) %copy-start) | copy-done | bytes 1638424
  2.1 0.0 copy-start.1
  2.1 1.4 %copy-done.1 = bf16[1,640,1280]{2,1,0:T(8,128)(2,1)S(1)} copy-done((bf16[1,640,1280]{2,1,0:T(8,128)(2,1)S(1)}, bf16[1,640,1280]{2,1,0:T(8,128)(2,1)}, u32[]{:S(2)}) %copy-start.1) | copy-done | bytes 1638424
  3.5 0.0 copy-start.2
  3.5 1.0 copy-done.2
  4.5 0.0 copy-start.3
  4.5 1.0 copy-done.3
  5.4 0.0 copy-start.4
  5.4 1.0 copy-done.4
  6.4 101.7 %shard_map.68 = (bf16[128,1280]{1,0:T(8,128)(2,1)S(1)}, bf16[40,8]{1,0:T(8,128)(2,1)S(1)}) custom-call(bf16[128,1280]{1,0:T(8,128)(2,1)S(1)} %copy-done.2, bf16[128,1280]{1,0:T(8,128)(2,1)S(1)} %copy-done.3, bf16[1280,128]{1,0:T(8,128)(2,1)S(1)} %copy-done.4, bf16[1,640,1280]{2,1,0:T(8,128)(2,1)S(1)} %copy-done, bf16[1,640,1280]{2,1,0:T(8,128)(2,1)S(1)} %copy-done.1), custom_call_target="tpu_custom_call" | custom-call | tf_op jit(solution)/shard_map/pallas_call | solution.py:371
  108.2 0.7 copy.7
  108.8 0.7 copy.9
Async XLA Ops:
  0.6 1.4 %copy-start = (bf16[1,640,1280]{2,1,0:T(8,128)(2,1)S(1)}, bf16[1,640,1280]{2,1,0:T(8,128)(2,1)}, u32[]{:S(2)}) copy-start(bf16[1,640,1280]{2,1,0:T(8,128)(2,1)} %w1_hbm.1) | copy-start | bytes 4915204
  2.1 1.4 %copy-start.1 = (bf16[1,640,1280]{2,1,0:T(8,128)(2,1)S(1)}, bf16[1,640,1280]{2,1,0:T(8,128)(2,1)}, u32[]{:S(2)}) copy-start(bf16[1,640,1280]{2,1,0:T(8,128)(2,1)} %w2_hbm.1) | copy-start | bytes 4915204
  3.5 1.0 copy-start.2
  4.5 1.0 copy-start.3
  5.4 1.0 copy-start.4

commit v3 on v2

v3 whole, which is shorter than its diff:
```python
import functools

import jax
import jax.numpy as jnp
from jax import lax
from jax.experimental import pallas as pl
from jax.experimental.pallas import tpu as pltpu
from jax.sharding import PartitionSpec as P

MESH = pl.DeviceIdType.MESH
PLANE_Y = 4
GROUPS = ((4, 8), (0, 4))
LOOK = True

gelu_scale = 0.7978845608
gelu_cubic = 0.044715

F32 = jnp.float32
BF16 = jnp.bfloat16


def gelu_parts(pre_act):
    inner_arg = gelu_scale * (pre_act + gelu_cubic * pre_act * pre_act * pre_act)
    tangent = jnp.tanh(inner_arg)
    gelu_value = 0.5 * pre_act * (1.0 + tangent)
    gelu_slope = 0.5 * (1.0 + tangent) + 0.5 * pre_act * (1.0 - tangent * tangent) * gelu_scale * (
        1.0 + 3.0 * gelu_cubic * pre_act * pre_act
    )
    return (gelu_value, gelu_slope)


def dot(a, b, ca, cb):
    return lax.dot_general(a, b, (((ca,), (cb,)), ((), ())), preferred_element_type=F32)


def tiles(extent, step=256):
    return [(at, min(step, extent - at)) for at in range(0, extent, step)]


def up16(n):
    return -(-n // 16) * 16


def log2(n):
    return n.bit_length() - 1


def kernel(
    nx, ny, zl_n,
    tok_hbm, og_hbm, sp_hbm, w1_hbm, w2_hbm,
    tg_ref, pg_ref,
    tok, og, sp, w1, w2, spt, tokt, disp, comb, disp_b, lg_b,
    s_buf, r_buf, t_buf, x_buf, gv, pgd, p_buf, o_send, o_recv, u_buf, v_buf, q_buf, b_buf, c_buf, g_buf,
    back_buf, pg_send, pg_recv, pad, f2_send, f2_recv,
    load_sem, swap_s, swap_r, p1_s, p1_r, p2_s, p2_r, rl_s, dd_s, dd_r, o_s, o_r,
    v_s, v_r, b_s, b_r, g_s, g_r, gd_s, gd_r, f1_s, f1_r, f2_s, f2_r,
):
    plane, ring, pairs = nx * ny, 2 * zl_n, zl_n
    reach = pairs - 1
    at_dp, at_ex = lax.axis_index("dp"), lax.axis_index("expert")
    core, zl = lax.rem(at_ex, 2), lax.div(at_ex, 2)
    y, xz = lax.rem(at_dp, ny), lax.div(at_dp, ny)
    zh, x = lax.rem(xz, 2), lax.div(xz, 2)
    z, xy = zh * zl_n + zl, x * ny + y
    sign = 2 * lax.rem(z, 2) - 1
    pair = lax.div(z, 2)
    other = 1 - core

    def turn(v):
        return lax.rem(v + 2 * ring, ring)

    def shift(j):
        return lax.rem(xy + j, plane)

    def device(xy_to, z_to, core_to):
        x_to, y_to = lax.div(xy_to, ny), lax.rem(xy_to, ny)
        return (
            (x_to * 2 + lax.div(z_to, zl_n)) * ny + y_to,
            lax.rem(z_to, zl_n) * 2 + core_to,
        )

    partner = device(xy, z, other)
    sibling = device(xy, turn(z - sign), core)
    started = []

    def send(src, dst, send_sem, recv_sem, to):
        copy = pltpu.make_async_remote_copy(
            src_ref=src, dst_ref=dst, send_sem=send_sem, recv_sem=recv_sem,
            device_id=to, device_id_type=MESH,
        )
        copy.start()
        started.append(copy)

    def arrived(dst, recv_sem):
        pltpu.make_async_remote_copy(
            src_ref=dst, dst_ref=dst, send_sem=recv_sem, recv_sem=recv_sem,
            device_id=partner, device_id_type=MESH,
        ).wait_recv()

    rows, width = tok_hbm.shape
    half = width // 2
    image = 2 * rows
    slots = plane * pairs
    own_cols = pl.ds(pl.multiple_of(core * half, half), half)

    barrier = pltpu.get_barrier_semaphore()
    pl.semaphore_signal(barrier, inc=1, device_id=partner, device_id_type=MESH)
    for j in range(1, plane):
        pl.semaphore_signal(barrier, inc=1, device_id=device(shift(j), z, core), device_id_type=MESH)
    for j in range(1, ring):
        for to in range(2):
            pl.semaphore_signal(
                barrier, inc=1, device_id=device(xy, turn(z + j), to), device_id_type=MESH
            )

    loads = [
        pltpu.make_async_copy(src, dst, load_sem.at[i])
        for i, (src, dst) in enumerate(
            [(tok_hbm, tok.at[core]), (og_hbm, og.at[core]), (sp_hbm, sp), (w1_hbm.at[0], w1), (w2_hbm.at[0], w2)]
        )
    ]
    for load in loads:
        load.start()

    place = lax.broadcasted_iota(jnp.int32, (slots, slots), 0)
    zl2_n = pairs // 2
    of_place = (
        (place >> log2(pairs * ny)) * (2 * ny * zl2_n)
        + ((place >> log2(zl2_n)) & 1) * (ny * zl2_n)
        + ((place >> log2(pairs)) & (ny - 1)) * zl2_n
        + (place & (zl2_n - 1))
    )
    across = lax.broadcasted_iota(jnp.int32, (slots, slots), 1)
    slot_order = (across == of_place).astype(F32).astype(BF16)
    cells = 2 * slots
    first_at = lax.broadcasted_iota(jnp.int32, (cells, cells), 0)
    second_at = lax.broadcasted_iota(jnp.int32, (cells, cells), 1)

    def by_source(at):
        kind = (at >> log2(plane)) & 1
        return (at & (plane - 1)) * (2 * pairs) + kind * pairs + (at >> log2(2 * plane))

    to_pairs = (second_at == by_source(first_at)).astype(F32).astype(BF16)
    to_sources = (first_at == by_source(second_at)).astype(F32).astype(BF16)
    pg_send[...] = jnp.zeros_like(pg_send)
    loads[2].wait()
    spt[...] = dot(slot_order, sp[...], 1, 1).astype(BF16)
    loads[0].wait()
    loads[1].wait()

    pl.semaphore_wait(barrier, plane + 2 * (ring - 1))
    send(tok.at[core], tok.at[core], swap_s.at[0], swap_r.at[0], partner)
    send(og.at[core], og.at[core], swap_s.at[1], swap_r.at[1], partner)
    arrived(tok.at[other], swap_r.at[0])

    tok_all = tok[...].reshape(image, width)
    logits = dot(spt[...], tok_all, 1, 1)
    col_exp = jnp.exp(logits - jnp.max(logits, axis=1, keepdims=True))
    dispatch = col_exp / jnp.sum(col_exp, axis=1, keepdims=True)
    disp[...] = dispatch
    disp_b[...] = dispatch.astype(BF16)
    slot_in = dot(disp_b[...], tok[:, :, own_cols].reshape(image, half), 1, 0)
    row_exp = jnp.exp(logits - jnp.max(logits, axis=0, keepdims=True))
    combine = row_exp / jnp.sum(row_exp, axis=0, keepdims=True)
    comb[...] = combine
    arrived(og.at[other], swap_r.at[1])
    slot_grad = dot(combine.astype(BF16), og[:, :, own_cols].reshape(image, half), 1, 0)
    s_buf[...] = jnp.concatenate(
        [slot_in.reshape(plane, pairs, half), slot_grad.reshape(plane, pairs, half)], axis=1
    ).astype(BF16)

    for j in range(1, plane):
        to = shift(j)
        send(s_buf.at[to], r_buf.at[xy], p1_s.at[j], p1_r.at[xy], device(to, z, core))
    r_buf[xy] = s_buf[xy]
    for j in range(1, plane):
        arrived(r_buf.at[shift(j)], p1_r.at[shift(j)])
    t_buf[...] = dot(to_pairs, r_buf[...].reshape(cells, half), 1, 0).astype(BF16).reshape(
        pairs, 2, plane, half
    )

    hops = [(sign, d) for d in range(1, pairs, 2)] + [(-sign, d) for d in range(2, pairs, 2)]
    hops.sort(key=lambda hop: -hop[1])
    for way, d in hops:
        to = turn(z + way * d)
        send(
            t_buf.at[lax.div(to, 2)], x_buf.at[core, :, 2 * d], p2_s.at[d], p2_r.at[2 * d],
            device(xy, to, core),
        )
    mine = t_buf.at[pair]
    send(mine, x_buf.at[core, :, 1], p2_s.at[0], p2_r.at[1], sibling)
    send(mine, x_buf.at[core, :, 0], dd_s.at[0], dd_r.at[0], partner)
    x_buf[core, :, 0] = t_buf[pair]
    images = ring * plane
    hidden = w1.shape[0]

    def take(at):
        slot = x_buf.at[core, :, at]
        arrived(slot, p2_r.at[at])
        if at > 1 and at % 2 == 0:
            send(slot, x_buf.at[core, :, at + 1], rl_s.at[at // 2], p2_r.at[at + 1], sibling)
        send(slot, slot, dd_s.at[at], dd_r.at[at], partner)

    def take_first(low, high):
        for j in range(high - 1, max(low, 1) - 1, -1):
            take(2 * j)

    def take_relayed(low, high):
        for j in range(high - 1, low - 1, -1):
            take(2 * j + 1)
        for at in range(2 * low, 2 * high):
            arrived(x_buf.at[other, :, at], dd_r.at[at])

    def expert(low, high):
        count = (high - low) * 2 * plane
        span = slice(2 * low, 2 * high)

        def both(kind, weights, at, n):
            return sum(
                dot(x_buf[h, kind, span].reshape(count, half), weights[at : at + n, h * half : (h + 1) * half], 1, 1)
                for h in range(2)
            )

        for at, n in tiles(hidden):
            gelu_value, gelu_slope = gelu_parts(both(0, w1, at, n))
            gv[:count, at : at + n] = gelu_value.astype(BF16)
            pgd[:count, at : at + n] = (both(1, w2, at, n) * gelu_slope).astype(BF16)

        def product(kind, whose, at, n):
            left, right = ((gv, w2), (pgd, w1))[kind]
            cols = pl.ds(pl.multiple_of(whose * half + at, 128), n)
            return dot(left[:count], right[:, cols], 1, 0).reshape(2 * (high - low), plane, n)

        for kind in range(2):
            for at, n in tiles(half):
                o_send[kind, span, :, at : at + n] = product(kind, other, at, n).astype(BF16)
        send(o_send.at[:, span], o_recv.at[:, span], o_s.at[low], o_r.at[low], partner)
        for kind in range(2):
            for at, n in tiles(half):
                p_buf[kind, span, :, at : at + n] = product(kind, core, at, n)

    def give(low, high):
        span = slice(2 * low, 2 * high)
        arrived(o_recv.at[:, span], o_r.at[low])
        for j in range(high - 1, low - 1, -1):
            at = 2 * j + 1
            u_buf[j] = (p_buf[:, at] + o_recv[:, at].astype(F32)).astype(BF16)
            send(u_buf.at[j], v_buf.at[j], v_s.at[j], v_r.at[j], sibling)

    def pass_back(low, high):
        for j in range(high - 1, low - 1, -1):
            arrived(v_buf.at[j], v_r.at[j])
            at = 2 * j
            whole = (p_buf[:, at] + o_recv[:, at].astype(F32) + v_buf[j].astype(F32)).astype(BF16)
            if j == 0:
                b_buf[pair] = whole
            else:
                q_buf[j] = whole
                send(q_buf.at[j], b_buf.at[pair], b_s.at[j], b_r.at[pair], device(xy, turn(z + sign * j), core))

    groups = [(low, min(high, pairs)) for low, high in GROUPS if low < pairs]
    take_first(*groups[0])
    for i, group in enumerate(groups):
        if LOOK and i + 1 < len(groups):
            take_first(*groups[i + 1])
        take_relayed(*group)
        if i == 0:
            loads[3].wait()
            loads[4].wait()
        expert(*group)
        if not LOOK and i + 1 < len(groups):
            take_first(*groups[i + 1])
        if i > 0:
            pass_back(*groups[i - 1])
        give(*group)
    pass_back(*groups[-1])

    for at, n in tiles(width, 128):
        tokt[at : at + n] = tok[:, :, at : at + n].reshape(image, n).astype(F32).T.astype(BF16)

    for j in range(1, pairs):
        src = lax.rem(pair + j, pairs)
        arrived(b_buf.at[src], b_r.at[src])
    c_buf[...] = dot(to_sources, b_buf[...].reshape(cells, half), 1, 0).astype(BF16).reshape(
        plane, 2 * pairs, half
    )

    for j in range(1, plane):
        to = shift(j)
        send(c_buf.at[to], g_buf.at[xy], g_s.at[j], g_r.at[xy], device(to, z, core))
    g_buf[xy] = c_buf[xy]
    for j in range(1, plane):
        src = shift(plane - j)
        arrived(g_buf.at[src], g_r.at[src])
    came = g_buf[...].astype(F32)
    for kind in (1, 0):
        back_buf[kind, core] = came[:, kind * pairs : (kind + 1) * pairs].reshape(slots, half).astype(BF16)
        mine = back_buf.at[kind, core]
        send(mine, mine, gd_s.at[kind], gd_r.at[kind], partner)

    def inner(kind, against):
        arrived(back_buf.at[kind, other], gd_r.at[kind])
        return sum(
            dot(back_buf[kind, h], against[:, :, h * half : (h + 1) * half].reshape(image, half), 1, 1)
            for h in range(2)
        )

    disp_grad = inner(1, tok)
    comb_grad = inner(0, og)
    combine = comb[...]
    dispatch = disp[...]
    comb_inner = jnp.sum(combine * comb_grad, axis=0, keepdims=True)
    logit_grad = combine * (comb_grad - comb_inner) + dispatch * (disp_grad - jnp.sum(dispatch * disp_grad, axis=1, keepdims=True))
    lg_b[...] = logit_grad.astype(BF16)

    in_order = dot(lg_b[...], slot_order, 0, 0).astype(BF16)
    block = width // (2 * plane)
    for x_to in range(nx):
        strip_at = pl.ds(pl.multiple_of(x_to * 2 * ny * block + core * ny * block, 16), ny * block)
        pg_send[x_to * ny : (x_to + 1) * ny, :block] = (
            dot(tokt[strip_at, :], in_order, 1, 0).reshape(ny, block, slots).astype(BF16)
        )
    for j in range(1, plane):
        to = shift(j)
        send(pg_send.at[to], pg_recv.at[xy], f1_s.at[j], f1_r.at[xy], device(to, z, core))

    own_rows = pl.ds(pl.multiple_of(core * rows, rows), rows)
    for h in range(2):
        cols = slice(h * half, (h + 1) * half)
        tg_ref[:, cols] = (
            dot(disp_b[:, own_rows], back_buf[1, h], 0, 0) + dot(lg_b[:, own_rows], spt[:, cols], 0, 0)
        ).astype(BF16)

    total = pg_send[xy].astype(F32)
    for j in range(1, plane):
        src = shift(plane - j)
        arrived(pg_recv.at[src], f1_r.at[src])
        total = total + pg_recv[src].astype(F32)
    pad[...] = jnp.zeros_like(pad)
    pad[:block, :slots] = total[:block]
    per = slots // ring
    f2_send[...] = pad[...].T[:slots].reshape(ring, per, pad.shape[0])

    for j in sorted(range(1, ring), key=lambda j: -min(j, ring - j)):
        to = turn(at_ex + j)
        send(
            f2_send.at[to], f2_recv.at[z], f2_s.at[j], f2_r.at[z],
            device(xy, core * zl_n + lax.div(to, 2), lax.rem(to, 2)),
        )
    stays = zh == core

    def away(start):
        copy = pltpu.make_async_remote_copy(
            src_ref=f2_send.at[at_ex], dst_ref=f2_recv.at[z], send_sem=f2_s.at[0], recv_sem=f2_r.at[z],
            device_id=device(xy, core * zl_n + zl, core), device_id_type=MESH,
        )
        if start:
            copy.start()
        else:
            copy.wait_send()

    @pl.when(stays)
    def _():
        f2_recv[z] = f2_send[at_ex]

    @pl.when(jnp.logical_not(stays))
    def _():
        away(True)
        arrived(f2_recv.at[z], f2_r.at[z])

    for j in range(1, ring):
        src = turn(z + j)
        arrived(f2_recv.at[src], f2_r.at[src])
    pg_ref[...] = jnp.sum(f2_recv[...], axis=0)[:, :block].astype(BF16)

    @pl.when(jnp.logical_not(stays))
    def _():
        away(False)

    for copy in started:
        copy.wait_send()


def shards(ny, tokens, out_grad, slot_param, w_in, w_out):
    dp, ex = lax.axis_size("dp"), lax.axis_size("expert")
    nx, zl_n = dp // (2 * ny), ex // 2
    plane, ring, pairs = nx * ny, 2 * zl_n, zl_n
    rows, width = tokens.shape
    slots = slot_param.shape[1]
    hidden = w_in.shape[1]
    half, image, images = width // 2, 2 * rows, ring * plane
    block, per = width // dp, slots // ex
    side = max(128, slots)
    dma = pltpu.SemaphoreType.DMA
    vmem = pltpu.VMEM
    token_grad, param_grad = pl.pallas_call(
        functools.partial(kernel, nx, ny, zl_n),
        out_shape=(
            jax.ShapeDtypeStruct((rows, width), BF16),
            jax.ShapeDtypeStruct((per, block), BF16),
        ),
        in_specs=[pl.BlockSpec(memory_space=pl.ANY)] * 5,
        out_specs=(pl.BlockSpec(memory_space=pltpu.VMEM),) * 2,
        scratch_shapes=[
            vmem((2, rows, width), BF16),
            vmem((2, rows, width), BF16),
            vmem((width, slots), BF16),
            vmem((hidden, width), BF16),
            vmem((hidden, width), BF16),
            vmem((slots, width), BF16),
            vmem((width, image), BF16),
            vmem((slots, image), F32),
            vmem((slots, image), F32),
            vmem((slots, image), BF16),
            vmem((slots, image), BF16),
            vmem((plane, 2 * pairs, half), BF16),
            vmem((plane, 2 * pairs, half), BF16),
            vmem((pairs, 2, plane, half), BF16),
            vmem((2, 2, ring, plane, half), BF16),
            vmem((images, hidden), BF16),
            vmem((images, hidden), BF16),
            vmem((2, ring, plane, half), F32),
            vmem((2, ring, plane, half), BF16),
            vmem((2, ring, plane, half), BF16),
            vmem((pairs, 2, plane, half), BF16),
            vmem((pairs, 2, plane, half), BF16),
            vmem((pairs, 2, plane, half), BF16),
            vmem((pairs, 2, plane, half), BF16),
            vmem((plane, 2 * pairs, half), BF16),
            vmem((plane, 2 * pairs, half), BF16),
            vmem((2, 2, slots, half), BF16),
            vmem((plane, up16(block), slots), BF16),
            vmem((plane, up16(block), slots), BF16),
            vmem((side, side), F32),
            vmem((ring, per, side), F32),
            vmem((ring, per, side), F32),
            dma((5,)),
            dma((2,)), dma((2,)),
            dma((plane,)), dma((plane,)),
            dma((pairs,)), dma((ring,)), dma((pairs,)),
            dma((ring,)), dma((ring,)),
            dma((pairs,)), dma((pairs,)),
            dma((pairs,)), dma((pairs,)),
            dma((pairs,)), dma((pairs,)),
            dma((plane,)), dma((plane,)),
            dma((2,)), dma((2,)),
            dma((plane,)), dma((plane,)),
            dma((ring,)), dma((ring,)),
        ],
        compiler_params=pltpu.CompilerParams(
            collective_id=0, has_side_effects=True, vmem_limit_bytes=60 << 20
        ),
    )(tokens, out_grad, slot_param, w_in, w_out)
    return token_grad, param_grad.T


def solution(mesh):
    placed = (
        P(("dp", "expert"), None),
        P(("dp", "expert"), None),
        P(),
        P(("dp", "expert"), None, None),
        P(("dp", "expert"), None, None),
    )
    return jax.shard_map(
        functools.partial(shards, PLANE_Y),
        mesh=mesh,
        in_specs=placed,
        out_specs=(P(("dp", "expert"), None), P("dp", "expert")),
        check_vma=False,
    )
```

time: 110 us -> 101 us (0.918)
  Pallas kernels: 102 us -> 96.8 us
  local copies, waits for them, and re-layouts: 7.15 us -> 2.97 us
    pallas_call x1, Pallas kernels: 102 us -> 96.8 us  [shards(): pl.pallas_call(functools.partial(kernel, nx, ny, zl_n), out_shape=(jax.Sh...]
    unnamed x11 -> x2, local copies, waits for them, and re-layouts: 6.49 us -> 2.97 us
where the time goes in v3:
time: 101 us; the launch traced here: 100 us
  Pallas kernels  96.8 us (96%)
  local copies, waits for them, and re-layouts  2.97 us (3%)
    pallas_call x1, Pallas kernels, shards(): pl.pallas_call(functools.partial(kernel, nx, ny, zl_n), out_shape=(jax.Sh...  96.8 us
    unnamed x2, local copies, waits for them, and re-layouts  2.97 us

profile of v3, /device:TPU:1, one launch (start us, length us, event | category | flops | bytes accessed | tf_op | source)
XLA Modules:
  0.0 100.4 jit_solution(4713246840580100730)
XLA Ops:
  0.6 96.8 %shard_map.68 = (bf16[128,1280]{1,0:T(8,128)(2,1)}, bf16[8,40]{1,0:T(8,128)(2,1)}) custom-call(bf16[128,1280]{1,0:T(8,128)(2,1)} %tok_hbm.1, bf16[128,1280]{1,0:T(8,128)(2,1)} %og_hbm.1, bf16[1280,128]{1,0:T(8,128)(2,1)} %sp_hbm.1, bf16[1,640,1280]{2,1,0:T(8,128)(2,1)} %w1_hbm.1, bf16[1,640,1280]{2,1,0:T(8,128)(2,1)} %w2_hbm.1), custom_call_target="tpu_custom_call" | custom-call | tf_op jit(solution)/shard_map/pallas_call | solution.py:396
  97.4 1.7 %copy.9 = bf16[128,1280]{1,0:T(8,128)(2,1)} copy(bf16[128,1280]{1,0:T(8,128)(2,1)} %get-tuple-element.8) | data formatting | bytes 655360
  99.1 1.3 %copy.10 = bf16[40,8]{0,1:T(8,128)(2,1)} copy(bf16[40,8]{0,1:T(8,128)(2,1)} %bitcast.1) | data formatting | bytes 1280

commit v4 on v3

--- a/solution.py
+++ b/solution.py
@@ -53,7 +53,7 @@
     s_buf, r_buf, t_buf, x_buf, gv, pgd, p_buf, o_send, o_recv, u_buf, v_buf, q_buf, b_buf, c_buf, g_buf,
     back_buf, pg_send, pg_recv, pad, f2_send, f2_recv,
     load_sem, swap_s, swap_r, p1_s, p1_r, p2_s, p2_r, rl_s, dd_s, dd_r, o_s, o_r,
-    v_s, v_r, b_s, b_r, g_s, g_r, gd_s, gd_r, f1_s, f1_r, f2_s, f2_r,
+    v_s, v_r, b_s, b_r, g_s, g_r, gd_s, gd_r, f1_s, f1_r, f2_s, f2_r, known,
 ):
     plane, ring, pairs = nx * ny, 2 * zl_n, zl_n
     reach = pairs - 1
@@ -107,12 +107,16 @@
     pl.semaphore_signal(barrier, inc=1, device_id=partner, device_id_type=MESH)
     for j in range(1, plane):
         pl.semaphore_signal(barrier, inc=1, device_id=device(shift(j), z, core), device_id_type=MESH)
-    for j in range(1, ring):
-        for to in range(2):
+    for step in (1, ring - 1):
+        pl.semaphore_signal(barrier, inc=1, device_id=device(xy, turn(z + step), core), device_id_type=MESH)
+
+    def tell(i):
+        for step in (1 << i, ring - (1 << i)):
             pl.semaphore_signal(
-                barrier, inc=1, device_id=device(xy, turn(z + j), to), device_id_type=MESH
+                known.at[i], inc=1, device_id=device(xy, turn(z + step), core), device_id_type=MESH
             )
 
+    rounds = log2(ring) - 1
     loads = [
         pltpu.make_async_copy(src, dst, load_sem.at[i])
         for i, (src, dst) in enumerate(
@@ -148,7 +152,8 @@
     loads[0].wait()
     loads[1].wait()
 
-    pl.semaphore_wait(barrier, plane + 2 * (ring - 1))
+    pl.semaphore_wait(barrier, plane + 2)
+    tell(0)
     send(tok.at[core], tok.at[core], swap_s.at[0], swap_r.at[0], partner)
     send(og.at[core], og.at[core], swap_s.at[1], swap_r.at[1], partner)
     arrived(tok.at[other], swap_r.at[0])
@@ -173,11 +178,15 @@
         to = shift(j)
         send(s_buf.at[to], r_buf.at[xy], p1_s.at[j], p1_r.at[xy], device(to, z, core))
     r_buf[xy] = s_buf[xy]
+    for i in range(1, rounds):
+        pl.semaphore_wait(known.at[i - 1], 2)
+        tell(i)
     for j in range(1, plane):
         arrived(r_buf.at[shift(j)], p1_r.at[shift(j)])
     t_buf[...] = dot(to_pairs, r_buf[...].reshape(cells, half), 1, 0).astype(BF16).reshape(
         pairs, 2, plane, half
     )
+    pl.semaphore_wait(known.at[rounds - 1], 2)
 
     hops = [(sign, d) for d in range(1, pairs, 2)] + [(-sign, d) for d in range(2, pairs, 2)]
     hops.sort(key=lambda hop: -hop[1])
@@ -446,6 +455,7 @@
             dma((2,)), dma((2,)),
             dma((plane,)), dma((plane,)),
             dma((ring,)), dma((ring,)),
+            pltpu.SemaphoreType.REGULAR((max(1, ring.bit_length() - 2),)),
         ],
         compiler_params=pltpu.CompilerParams(
             collective_id=0, has_side_effects=True, vmem_limit_bytes=60 << 20

time: 101 us -> 98.6 us (0.976)
  Pallas kernels: 96.8 us -> 94.8 us
    pallas_call x1, Pallas kernels: 96.8 us -> 94.8 us  [shards(): pl.pallas_call(functools.partial(kernel, nx, ny, zl_n), out_shape=(jax.Sh...]
where the time goes in v4:
time: 98.6 us; the launch traced here: 98.4 us
  Pallas kernels  94.8 us (96%)
  local copies, waits for them, and re-layouts  2.97 us (3%)
    pallas_call x1, Pallas kernels, shards(): pl.pallas_call(functools.partial(kernel, nx, ny, zl_n), out_shape=(jax.Sh...  94.8 us
    unnamed x2, local copies, waits for them, and re-layouts  2.97 us

profile of v4, /device:TPU:1, one launch (start us, length us, event | category | flops | bytes accessed | tf_op | source)
XLA Modules:
  0.0 98.4 jit_solution(6018255506198894198)
XLA Ops:
  0.6 94.8 %shard_map.68 = (bf16[128,1280]{1,0:T(8,128)(2,1)}, bf16[8,40]{1,0:T(8,128)(2,1)}) custom-call(bf16[128,1280]{1,0:T(8,128)(2,1)} %tok_hbm.1, bf16[128,1280]{1,0:T(8,128)(2,1)} %og_hbm.1, bf16[1280,128]{1,0:T(8,128)(2,1)} %sp_hbm.1, bf16[1,640,1280]{2,1,0:T(8,128)(2,1)} %w1_hbm.1, bf16[1,640,1280]{2,1,0:T(8,128)(2,1)} %w2_hbm.1), custom_call_target="tpu_custom_call" | custom-call | tf_op jit(solution)/shard_map/pallas_call | solution.py:405
  95.4 1.7 %copy.9 = bf16[128,1280]{1,0:T(8,128)(2,1)} copy(bf16[128,1280]{1,0:T(8,128)(2,1)} %get-tuple-element.8) | data formatting | bytes 655360
  97.1 1.3 %copy.10 = bf16[40,8]{0,1:T(8,128)(2,1)} copy(bf16[40,8]{0,1:T(8,128)(2,1)} %bitcast.1) | data formatting | bytes 1280

commit v5 on v4

--- a/solution.py
+++ b/solution.py
@@ -9,7 +9,7 @@
 
 MESH = pl.DeviceIdType.MESH
 PLANE_Y = 4
-GROUPS = ((4, 8), (0, 4))
+GROUPS = ((3, 8), (0, 3))
 LOOK = True
 
 gelu_scale = 0.7978845608
@@ -53,7 +53,7 @@
     s_buf, r_buf, t_buf, x_buf, gv, pgd, p_buf, o_send, o_recv, u_buf, v_buf, q_buf, b_buf, c_buf, g_buf,
     back_buf, pg_send, pg_recv, pad, f2_send, f2_recv,
     load_sem, swap_s, swap_r, p1_s, p1_r, p2_s, p2_r, rl_s, dd_s, dd_r, o_s, o_r,
-    v_s, v_r, b_s, b_r, g_s, g_r, gd_s, gd_r, f1_s, f1_r, f2_s, f2_r, known,
+    v_s, v_r, b_s, b_r, g_s, g_r, gd_s, gd_r, f1_s, f1_r, f2_s, f2_r, known, tg,
 ):
     plane, ring, pairs = nx * ny, 2 * zl_n, zl_n
     reach = pairs - 1
@@ -107,7 +107,8 @@
     pl.semaphore_signal(barrier, inc=1, device_id=partner, device_id_type=MESH)
     for j in range(1, plane):
         pl.semaphore_signal(barrier, inc=1, device_id=device(shift(j), z, core), device_id_type=MESH)
-    for step in (1, ring - 1):
+    near = 2 if ring >= 8 else 1
+    for step in [way for k in range(near) for way in (1 << k, ring - (1 << k))]:
         pl.semaphore_signal(barrier, inc=1, device_id=device(xy, turn(z + step), core), device_id_type=MESH)
 
     def tell(i):
@@ -152,8 +153,8 @@
     loads[0].wait()
     loads[1].wait()
 
-    pl.semaphore_wait(barrier, plane + 2)
-    tell(0)
+    pl.semaphore_wait(barrier, plane + 2 * near)
+    tell(near - 1)
     send(tok.at[core], tok.at[core], swap_s.at[0], swap_r.at[0], partner)
     send(og.at[core], og.at[core], swap_s.at[1], swap_r.at[1], partner)
     arrived(tok.at[other], swap_r.at[0])
@@ -178,7 +179,7 @@
         to = shift(j)
         send(s_buf.at[to], r_buf.at[xy], p1_s.at[j], p1_r.at[xy], device(to, z, core))
     r_buf[xy] = s_buf[xy]
-    for i in range(1, rounds):
+    for i in range(near, rounds):
         pl.semaphore_wait(known.at[i - 1], 2)
         tell(i)
     for j in range(1, plane):
@@ -279,10 +280,9 @@
         expert(*group)
         if not LOOK and i + 1 < len(groups):
             take_first(*groups[i + 1])
-        if i > 0:
-            pass_back(*groups[i - 1])
         give(*group)
-    pass_back(*groups[-1])
+    for group in groups:
+        pass_back(*group)
 
     for at, n in tiles(width, 128):
         tokt[at : at + n] = tok[:, :, at : at + n].reshape(image, n).astype(F32).T.astype(BF16)
@@ -336,9 +336,11 @@
     own_rows = pl.ds(pl.multiple_of(core * rows, rows), rows)
     for h in range(2):
         cols = slice(h * half, (h + 1) * half)
-        tg_ref[:, cols] = (
+        tg[:, cols] = (
             dot(disp_b[:, own_rows], back_buf[1, h], 0, 0) + dot(lg_b[:, own_rows], spt[:, cols], 0, 0)
         ).astype(BF16)
+    tg_out = pltpu.make_async_copy(tg, tg_ref, load_sem.at[5])
+    tg_out.start()
 
     total = pg_send[xy].astype(F32)
     for j in range(1, plane):
@@ -386,6 +388,7 @@
     def _():
         away(False)
 
+    tg_out.wait()
     for copy in started:
         copy.wait_send()
 
@@ -409,7 +412,7 @@
             jax.ShapeDtypeStruct((per, block), BF16),
         ),
         in_specs=[pl.BlockSpec(memory_space=pl.ANY)] * 5,
-        out_specs=(pl.BlockSpec(memory_space=pltpu.VMEM),) * 2,
+        out_specs=(pl.BlockSpec(memory_space=pl.ANY), pl.BlockSpec(memory_space=pltpu.VMEM)),
         scratch_shapes=[
             vmem((2, rows, width), BF16),
             vmem((2, rows, width), BF16),
@@ -443,7 +446,7 @@
             vmem((side, side), F32),
             vmem((ring, per, side), F32),
             vmem((ring, per, side), F32),
-            dma((5,)),
+            dma((6,)),
             dma((2,)), dma((2,)),
             dma((plane,)), dma((plane,)),
             dma((pairs,)), dma((ring,)), dma((pairs,)),
@@ -456,6 +459,7 @@
             dma((plane,)), dma((plane,)),
             dma((ring,)), dma((ring,)),
             pltpu.SemaphoreType.REGULAR((max(1, ring.bit_length() - 2),)),
+            vmem((rows, width), BF16),
         ],
         compiler_params=pltpu.CompilerParams(
             collective_id=0, has_side_effects=True, vmem_limit_bytes=60 << 20

time: 98.6 us -> 99.1 us (level)
  no operation moved by 1% of the time
where the time goes in v5:
time: 99.1 us; the launch traced here: 98.9 us
  Pallas kernels  95.3 us (96%)
  local copies, waits for them, and re-layouts  2.97 us (3%)
    pallas_call x1, Pallas kernels, shards(): pl.pallas_call(functools.partial(kernel, nx, ny, zl_n), out_shape=(jax.Sh...  95.3 us
    unnamed x2, local copies, waits for them, and re-layouts  2.97 us

profile of v5, /device:TPU:1, one launch (start us, length us, event | category | flops | bytes accessed | tf_op | source)
XLA Modules:
  0.0 98.9 jit_solution(4919132931331019621)
XLA Ops:
  0.6 95.3 %shard_map.68 = (bf16[128,1280]{1,0:T(8,128)(2,1)}, bf16[8,40]{1,0:T(8,128)(2,1)}) custom-call(bf16[128,1280]{1,0:T(8,128)(2,1)} %tok_hbm.1, bf16[128,1280]{1,0:T(8,128)(2,1)} %og_hbm.1, bf16[1280,128]{1,0:T(8,128)(2,1)} %sp_hbm.1, bf16[1,640,1280]{2,1,0:T(8,128)(2,1)} %w1_hbm.1, bf16[1,640,1280]{2,1,0:T(8,128)(2,1)} %w2_hbm.1), custom_call_target="tpu_custom_call" | custom-call | tf_op jit(solution)/shard_map/pallas_call | solution.py:408
  95.9 1.7 %copy.9 = bf16[128,1280]{1,0:T(8,128)(2,1)} copy(bf16[128,1280]{1,0:T(8,128)(2,1)} %get-tuple-element.8) | data formatting | bytes 655360
  97.6 1.3 %copy.10 = bf16[40,8]{0,1:T(8,128)(2,1)} copy(bf16[40,8]{0,1:T(8,128)(2,1)} %bitcast.1) | data formatting | bytes 1280
